TPU v7x, 32 devices: a whole 2x2x4 slice. The times are simulated.
32 devices in a mesh: depth: 4 (over y, core), lat: 8 (over z, x).
Axes of the slice: x: 2, y: 2, z: 4, core: 2. Of those that a mesh axis runs over, the one named last changes fastest.
Arguments:
- potential: float32 [2, 4, 2, 1024, 2048], P(None, 'depth', None, 'lat'), may hold values from -3 to 3, as said below
- incident: float32 [2, 2, 1024, 1024], P(None, None, 'lat'), may hold values from -6 to 6
- measured: float32 [2, 1024, 1024], P(None, 'lat'), may hold values from 0 to 3
- offsets: int32 [2, 2], replicated, may hold values from 0 to 1024, as said below
- kernel: bfloat16 [2, 9], replicated, may hold values from -1 to 1
Outputs:
- potential_grad: float32 [2, 4, 2, 1024, 2048], P(None, 'depth', None, 'lat')
Inputs may be any that keep to these rules, and one draw needn't show every extreme that they name: Row offsets are multiples of 128 from 0 to 1024; column offsets run from 0 to 1024. `potential`: part 0 (phase) lies in -3 to 3; part 1 (absorption) lies in 0.004 to 0.05.
All inputs are finite; a program needn't handle non-finite values.
Results may differ from a plain program's by a relative error of at most 0.038.
Values may be sent and summed in bfloat16 or wider, within the bound.
A program may use at most 64 MiB of HBM per device.

v0:
```python
import jax
import jax.numpy as jnp
from jax import lax
from jax.sharding import PartitionSpec as P


def with_halo(cells, sides, width):
    for axis, dim in sides:
        count = lax.axis_size(axis)
        head = lax.slice_in_dim(cells, 0, width, axis=dim)
        tail = lax.slice_in_dim(cells, cells.shape[dim] - width, cells.shape[dim], axis=dim)
        cells = jnp.concatenate(
            [
                lax.ppermute(tail, axis, [(i, (i + 1) % count) for i in range(count)]),
                cells,
                lax.ppermute(head, axis, [((i + 1) % count, i) for i in range(count)]),
            ],
            axis=dim,
        )
    return cells


def from_behind(array, axis, by):
    count = lax.axis_size(axis)
    pairs = [(i, i + by) for i in range(count) if 0 <= i + by < count]
    return lax.ppermute(array, axis, pairs)


def rounded(field_in):
    return lax.optimization_barrier(field_in.astype(jnp.bfloat16)).astype(jnp.float32)


def band_matrix(taps_re, taps_im, row_count, col_count, half_width, transposed):
    row_index = lax.broadcasted_iota(jnp.int32, (row_count, col_count), 0)
    col_index = lax.broadcasted_iota(jnp.int32, (row_count, col_count), 1)
    offset = row_index - col_index if transposed else col_index - row_index
    chooser = (offset[:, :, None] == jnp.arange(2 * half_width + 1, dtype=jnp.int32)).astype(
        jnp.float32
    )
    real_part = jnp.sum(chooser * taps_re, axis=2).astype(jnp.bfloat16)
    imag_part = jnp.sum(chooser * taps_im, axis=2).astype(jnp.bfloat16)
    return (real_part, imag_part)


def along_rows(field_in, real_mat, imag_mat):
    direct = jnp.einsum("rq,xpqc->xprc", real_mat, field_in, preferred_element_type=jnp.float32)
    crossed = jnp.einsum("rq,xpqc->xprc", imag_mat, field_in, preferred_element_type=jnp.float32)
    return jnp.stack([direct[0] - crossed[1], crossed[0] + direct[1]])


def along_cols(field_in, real_slab, imag_slab, half_width):
    columns = field_in.shape[-1]
    blocks = columns // 128
    padded = jnp.pad(field_in, ((0, 0), (0, 0), (0, 0), (half_width, 128 - half_width)))
    main_part = padded[..., :columns].reshape(field_in.shape[:-1] + (blocks, 128))
    extra_part = padded[..., 128 : columns + 128].reshape(field_in.shape[:-1] + (blocks, 128))[
        ..., : 2 * half_width
    ]
    slab_rows = jnp.concatenate([main_part, extra_part], axis=-1)
    direct = jnp.einsum("xprbq,qo->xprbo", slab_rows, real_slab, preferred_element_type=jnp.float32)
    crossed = jnp.einsum(
        "xprbq,qo->xprbo", slab_rows, imag_slab, preferred_element_type=jnp.float32
    )
    joined = jnp.stack([direct[0] - crossed[1], crossed[0] + direct[1]])
    return joined.reshape(field_in.shape)


def local(potential, incident, measured, offsets, kernel):
    lat_count = lax.axis_size("lat")
    depth_count = lax.axis_size("depth")
    lat_index = lax.axis_index("lat")
    depth_index = lax.axis_index("depth")
    band_rows = potential.shape[3]
    window = incident.shape[3]
    probe_count = incident.shape[1]
    half_width = (kernel.shape[1] - 1) // 2
    taps_re = kernel[0].astype(jnp.float32)
    taps_im = kernel[1].astype(jnp.float32)
    back_re = taps_re[::-1]
    back_im = -taps_im[::-1]
    row_pixel = offsets[:, 0]
    col_pixel = offsets[:, 1]
    first_band = row_pixel // band_rows
    place_band = (lat_index - first_band) % lat_count
    layer_pot = potential[:, 0]
    reach_steps = 2
    margin = reach_steps * half_width
    full_rows = band_rows + 2 * margin
    most_out = full_rows - 2 * half_width
    row_forward = band_matrix(taps_re, taps_im, most_out, full_rows, half_width, False)
    row_adjoint = band_matrix(back_re, back_im, most_out, full_rows, half_width, False)
    column_forward = band_matrix(taps_re, taps_im, 128 + 2 * half_width, 128, half_width, True)
    column_adjoint = band_matrix(back_re, back_im, 128 + 2 * half_width, 128, half_width, True)
    local_rows = jnp.arange(full_rows, dtype=jnp.int32) - margin
    window_row = place_band[:, None] * band_rows + local_rows[None, :]
    valid_rows = (window_row >= 0) & (window_row < window)
    keep_mask = valid_rows[None, :, :, None]
    padded_pot = with_halo(layer_pot, (("lat", 2),), margin)
    local_rows = jnp.arange(band_rows + 2 * margin, dtype=jnp.int32) - margin
    side_rows = (local_rows >= band_rows).astype(jnp.int32) - (local_rows < 0).astype(jnp.int32)
    halves = jnp.clip(
        (first_band[:, None] + place_band[:, None] + side_rows[None, :]) // lat_count, 0, 1
    )

    def cut_window(col_start):
        return lax.dynamic_slice_in_dim(padded_pot, col_start, window, 3)

    windows = jax.vmap(cut_window)(col_pixel)
    chosen = jnp.where((halves == 0)[:, None, :, None], windows[:, :, 0], windows[:, :, 1])
    damping = jnp.exp(-chosen[:, 1])
    phase_part = chosen[:, 0]
    transmit = jnp.stack([damping * jnp.cos(phase_part), damping * jnp.sin(phase_part)])

    def forward_segment(wave_ext, extent):
        low_row = margin - extent
        rows_in = band_rows + 2 * extent
        rows_out = rows_in - 2 * half_width
        factor = transmit[:, :, low_row : low_row + rows_in]
        inside = keep_mask[:, :, low_row : low_row + rows_in]
        values = wave_ext.astype(jnp.float32)
        product = jnp.stack(
            [
                factor[0] * values[0] - factor[1] * values[1],
                factor[0] * values[1] + factor[1] * values[0],
            ]
        )
        product = jnp.where(inside, product, 0.0).astype(jnp.bfloat16)
        spread = along_rows(
            product, row_forward[0][:rows_out, :rows_in], row_forward[1][:rows_out, :rows_in]
        ).astype(jnp.bfloat16)
        return along_cols(spread, column_forward[0], column_forward[1], half_width).astype(
            jnp.bfloat16
        )

    def backward_segment(adjoint, extent, entry):
        low_row = margin - extent
        rows_in = band_rows + 2 * extent
        rows_out = rows_in - 2 * half_width
        inside = keep_mask[:, :, low_row : low_row + rows_in]
        masked = jnp.where(inside, adjoint, jnp.zeros_like(adjoint))
        spread = along_cols(masked, column_adjoint[0], column_adjoint[1], half_width).astype(
            jnp.bfloat16
        )
        local_grad = rounded(
            along_rows(
                spread, row_adjoint[0][:rows_out, :rows_in], row_adjoint[1][:rows_out, :rows_in]
            )
        )
        factor = transmit[:, :, low_row + half_width : low_row + half_width + rows_out]
        earlier = jnp.stack(
            [
                factor[0] * local_grad[0] + factor[1] * local_grad[1],
                factor[0] * local_grad[1] - factor[1] * local_grad[0],
            ]
        ).astype(jnp.bfloat16)
        centre = extent - half_width
        own_rows = local_grad[:, :, centre : centre + band_rows]
        own_factor = factor[:, :, centre : centre + band_rows]
        entry_wave = entry.astype(jnp.float32)
        cross_re = entry_wave[0] * own_rows[0] + entry_wave[1] * own_rows[1]
        cross_im = entry_wave[0] * own_rows[1] - entry_wave[1] * own_rows[0]
        turned_re = own_factor[0] * cross_re + own_factor[1] * cross_im
        turned_im = own_factor[0] * cross_im - own_factor[1] * cross_re
        return (earlier, jnp.stack([turned_im, -turned_re]))

    start_wave = incident.astype(jnp.bfloat16)
    zeros_wave = jnp.zeros_like(start_wave)
    blocks = depth_count // reach_steps

    def forward_block(block_index, carry):
        moving, stored, leaving = carry
        entering = jnp.where(depth_index == 0, start_wave, moving)
        wave_ext = with_halo(entering, (("lat", 2),), margin)
        for sub_step in range(reach_steps):
            extent = margin - sub_step * half_width
            result = forward_segment(wave_ext, extent)
            active = depth_index == block_index * reach_steps + sub_step
            stored = jnp.where(active, wave_ext[:, :, extent : extent + band_rows], stored)
            if sub_step == reach_steps - 1:
                leaving = jnp.where(active, result, leaving)
            wave_ext = from_behind(result, "depth", 1)
        return (wave_ext, stored, leaving)

    moving, stored, leaving = lax.fori_loop(
        0, blocks, forward_block, (zeros_wave, zeros_wave, zeros_wave)
    )
    exit_vals = leaving.astype(jnp.float32)
    residual = exit_vals[0] * exit_vals[0] + exit_vals[1] * exit_vals[1] - measured
    seed_wave = (2.0 * residual[None] * exit_vals).astype(jnp.bfloat16)
    zeros_term = jnp.zeros(start_wave.shape, jnp.float32)

    def backward_block(block_index, carry):
        moving_back, collected = carry
        entering = jnp.where(depth_index == depth_count - 1, seed_wave, moving_back)
        adjoint = with_halo(entering, (("lat", 2),), margin)
        for sub_step in range(reach_steps):
            extent = margin - sub_step * half_width
            earlier, grad_term = backward_segment(adjoint, extent, stored)
            active = depth_index == depth_count - 1 - (block_index * reach_steps + sub_step)
            collected = jnp.where(active, grad_term, collected)
            adjoint = from_behind(earlier, "depth", -1)
        return (adjoint, collected)

    moving_back, gathered = lax.fori_loop(0, blocks, backward_block, (zeros_wave, zeros_term))
    own_half = (first_band + place_band) // lat_count
    gradient = jnp.zeros_like(layer_pot)

    def accumulate(probe_index, running):
        portion = lax.dynamic_index_in_dim(gathered, probe_index, 1, keepdims=False)
        zero_index = jnp.zeros((), jnp.int32)
        corner = (zero_index, own_half[probe_index], zero_index, col_pixel[probe_index])
        current = lax.dynamic_slice(running, corner, (2, 1, band_rows, window))
        return lax.dynamic_update_slice(running, current + portion[:, None], corner)

    gradient = lax.fori_loop(0, probe_count, accumulate, gradient)
    return gradient[:, None]


def solution(mesh):
    in_specs = (
        P(None, "depth", None, "lat", None),
        P(None, None, "lat", None),
        P(None, "lat", None),
        P(),
        P(),
    )
    out_specs = P(None, "depth", None, "lat", None)
    return jax.shard_map(local, mesh=mesh, in_specs=in_specs, out_specs=out_specs, check_vma=False)
```

profile of v0, /device:TPU:1, one launch (start us, length us, event | category | flops | bytes accessed | tf_op | source)
XLA Modules:
  0.0 383.3 jit_solution(11620859677189762755)
XLA Ops:
  4.0 3.0 collective-permute-start.9
  16.4 5.0 %pad_maximum_fusion.18 = f32[2,2,144,2048]{3,2,1,0:T(8,128)} fusion(f32[2,2,8,2048]{3,2,1,0:T(8,128)S(1)} %collective-permute-done.9, f32[2,2,128,2048]{3,2,1,0:T(8,128)} %bitcast.319, f32[2,2,8,2048]{3,2,1,0:T(8,128)S(1)} %collective-permute-done.8), kind=kLoop, calls=%fused_computation.154 | loop fusion | flops 2359296 | bytes 9437184 | tf_op jit(solution)/shard_map/concatenate | solution.py:12
  21.4 10.1 %while.53 = (s32[]{:T(128)}, f32[2,2,144,2048]{3,2,1,0:T(8,128)}, s32[2,4]{1,0:T(2,128)S(1)}, f32[2,2,2,144,1024]{4,3,0,1,2:T(8,128)}, s32[]{:T(128)}) while((s32[]{:T(128)}, f32[2,2,144,2048]{3,2,1,0:T(8,128)}, s32[2,4]{1,0:T(2,128)S(1)}, f32[2,2,2,144,1024]{4,3,0,1,2:T(8,128)}, s32[]{:T(128)}) %tuple.196), condition=%wide.while_cond, body=%wide.while_body.sunk | while | flops 2 | bytes 4719721 | solution.py:106
  22.0 4.5 %copy_dynamic-update-slice_fusion.2 = f32[2,2,2,144,1024]{4,3,0,1,2:T(8,128)} fusion(f32[2,2,2,144,1024]{4,3,0,1,2:T(8,128)} %get-tuple-element.1332, s32[]{:T(128)} %get-tuple-element.1329, f32[2,2,144,2048]{3,2,1,0:T(8,128)} %get-tuple-element.1335, s32[]{:T(128)} %bitcast.241), kind=kLoop, calls=%fused_computation.1.clone.1 | loop fusion | bytes 4719616 | tf_op jit(solution)/shard_map/vmap()/gather
  27.0 4.5 %copy_dynamic-update-slice_fusion.2 = f32[2,2,2,144,1024]{4,3,0,1,2:T(8,128)} fusion(f32[2,2,2,144,1024]{4,3,0,1,2:T(8,128)} %get-tuple-element.1332, s32[]{:T(128)} %get-tuple-element.1329, f32[2,2,144,2048]{3,2,1,0:T(8,128)} %get-tuple-element.1335, s32[]{:T(128)} %bitcast.241), kind=kLoop, calls=%fused_computation.1.clone.1 | loop fusion | bytes 4719616 | tf_op jit(solution)/shard_map/vmap()/gather
  34.2 5.7 %fusion.83 = (f32[2,144,1024]{2,1,0:T(8,128)}, f32[2,144,1024]{2,1,0:T(8,128)}, f32[1,2,144,1024]{3,2,1,0:T(8,128)S(1)}, f32[1,2,144,1024]{3,2,1,0:T(8,128)S(1)}) fusion(f32[2,2,144,1024]{3,2,0,1:T(8,128)S(1)} %bitcast_select_fusion), kind=kLoop, calls=%fused_computation.180 | loop fusion | flops 884736 | bytes 7077888 | tf_op jit(solution)/shard_map/mul | solution.py:112
  41.3 147.5 %while.54 = (s32[]{:T(128)}, bf16[2,2,128,1024]{3,2,1,0:T(8,128)(2,1)}, bf16[2,2,128,1024]{3,2,1,0:T(8,128)(2,1)}, bf16[2,2,128,1024]{3,2,1,0:T(8,128)(2,1)}, pr...) while((s32[]{:T(128)}, ...), condition=%wide.region_5.6_spmd.clone, body=%wide.region_4.5_spmd.clone.sunk | while | flops 1243172864 | bytes 121860712 | solution.py:184
  42.6 3.6 collective-permute-start
  47.6 4.5 %collective-permute-done.1 = bf16[2,2,8,1024]{3,2,1,0:T(8,128)(2,1)S(1)} collective-permute-done((bf16[2,2,8,1024]{3,2,1,0:T(8,128)(2,1)S(1)}, bf16[2,2,8,1024]{3,2,1,0:T(8,128)(2,1)S(1)}, u32[]{:S(2)}, u32[]{:S(2)}) %collective-permute-start.1) | collective-permute-done | bytes 65568 | tf_op jit(solution)/shard_map/while/body/eval_jaxpr/ppermute | solution.py:14
  66.3 6.0 %collective-permute-start.2 = (bf16[2,2,136,1024]{3,2,1,0:T(8,128)(2,1)}, bf16[2,2,136,1024]{3,2,1,0:T(8,128)(2,1)}, u32[]{:S(2)}, u32[]{:S(2)}) collective-permute-start(bf16[2,2,136,1024]{3,2,1,0:T(8,128)(2,1)} %pad_maximum_fusion.37), channel_id=1, source_target_pairs={{0,8},{8,16},{16,24},{1,9},{9,17},{17,25},{2,10},{10,18},{18,26},{... | collective-permute-start | bytes 3342344 | tf_op jit(solution)/shard_map/while/body/eval_jaxpr/ppermute | solution.py:26
  72.4 12.7 %collective-permute-done.2 = bf16[2,2,136,1024]{3,2,1,0:T(8,128)(2,1)} collective-permute-done((bf16[2,2,136,1024]{3,2,1,0:T(8,128)(2,1)}, bf16[2,2,136,1024]{3,2,1,0:T(8,128)(2,1)}, u32[]{:S(2)}, u32[]{:S(2)}) %collective-permute-start.2) | collective-permute-done | bytes 1114144 | tf_op jit(solution)/shard_map/while/body/eval_jaxpr/ppermute | solution.py:26
  100.5 4.4 %collective-permute-start.3 = (bf16[2,2,128,1024]{3,2,1,0:T(8,128)(2,1)}, bf16[2,2,128,1024]{3,2,1,0:T(8,128)(2,1)}, u32[]{:S(2)}, u32[]{:S(2)}) collective-permute-start(bf16[2,2,128,1024]{3,2,1,0:T(8,128)(2,1)} %get-tuple-element.1283), channel_id=1, source_target_pairs={{0,8},{8,16},{16,24},{1,9},{9,17},{17,25},{2,10},{10,18},{18,26},{... | collective-permute-start | bytes 3145736 | tf_op jit(solution)/shard_map/while/body/eval_jaxpr/ppermute | solution.py:26
  107.5 9.4 %collective-permute-done.3 = bf16[2,2,128,1024]{3,2,1,0:T(8,128)(2,1)} collective-permute-done((bf16[2,2,128,1024]{3,2,1,0:T(8,128)(2,1)}, bf16[2,2,128,1024]{3,2,1,0:T(8,128)(2,1)}, u32[]{:S(2)}, u32[]{:S(2)}) %collective-permute-start.3) | collective-permute-done | bytes 1048608 | tf_op jit(solution)/shard_map/while/body/eval_jaxpr/ppermute | solution.py:26
  121.4 2.8 collective-permute-done.1
  138.4 5.5 %collective-permute-start.2 = (bf16[2,2,136,1024]{3,2,1,0:T(8,128)(2,1)}, bf16[2,2,136,1024]{3,2,1,0:T(8,128)(2,1)}, u32[]{:S(2)}, u32[]{:S(2)}) collective-permute-start(bf16[2,2,136,1024]{3,2,1,0:T(8,128)(2,1)} %pad_maximum_fusion.37), channel_id=1, source_target_pairs={{0,8},{8,16},{16,24},{1,9},{9,17},{17,25},{2,10},{10,18},{18,26},{... | collective-permute-start | bytes 3342344 | tf_op jit(solution)/shard_map/while/body/eval_jaxpr/ppermute | solution.py:26
  144.0 12.7 %collective-permute-done.2 = bf16[2,2,136,1024]{3,2,1,0:T(8,128)(2,1)} collective-permute-done((bf16[2,2,136,1024]{3,2,1,0:T(8,128)(2,1)}, bf16[2,2,136,1024]{3,2,1,0:T(8,128)(2,1)}, u32[]{:S(2)}, u32[]{:S(2)}) %collective-permute-start.2) | collective-permute-done | bytes 1114144 | tf_op jit(solution)/shard_map/while/body/eval_jaxpr/ppermute | solution.py:26
  169.4 3.0 select_select_fusion.3
  172.4 4.4 %collective-permute-start.3 = (bf16[2,2,128,1024]{3,2,1,0:T(8,128)(2,1)}, bf16[2,2,128,1024]{3,2,1,0:T(8,128)(2,1)}, u32[]{:S(2)}, u32[]{:S(2)}) collective-permute-start(bf16[2,2,128,1024]{3,2,1,0:T(8,128)(2,1)} %get-tuple-element.1283), channel_id=1, source_target_pairs={{0,8},{8,16},{16,24},{1,9},{9,17},{17,25},{2,10},{10,18},{18,26},{... | collective-permute-start | bytes 3145736 | tf_op jit(solution)/shard_map/while/body/eval_jaxpr/ppermute | solution.py:26
  176.8 2.9 slice_select_fusion.2
  179.7 9.1 %collective-permute-done.3 = bf16[2,2,128,1024]{3,2,1,0:T(8,128)(2,1)} collective-permute-done((bf16[2,2,128,1024]{3,2,1,0:T(8,128)(2,1)}, bf16[2,2,128,1024]{3,2,1,0:T(8,128)(2,1)}, u32[]{:S(2)}, u32[]{:S(2)}) %collective-permute-start.3) | collective-permute-done | bytes 1048608 | tf_op jit(solution)/shard_map/while/body/eval_jaxpr/ppermute | solution.py:26
  194.0 161.1 %while.55 = (s32[]{:T(128)}, bf16[2,2,128,1024]{3,2,1,0:T(8,128)(2,1)}, f32[2,2,128,1024]{3,2,1,0:T(8,128)}, f32[2,2,144,1024]{3,2,1,0:T(8,128)S(1)}, pred[1,2,1...) while((s32[]{:T(128)}, ...), condition=%wide.region_11.12_spmd.clone, body=%wide.region_10.11_spmd.clone.sunk | while | flops 1266925568 | bytes 181284016 | solution.py:204
  221.1 15.1 %collective-permute-done.6 = bf16[2,2,136,1024]{3,2,1,0:T(8,128)(2,1)S(1)} collective-permute-done((bf16[2,2,136,1024]{3,2,1,0:T(8,128)(2,1)S(1)}, bf16[2,2,136,1024]{3,2,1,0:T(8,128)(2,1)S(1)}, u32[]{:S(2)}, u32[]{:S(2)}) %collective-permute-start.6) | collective-permute-done | bytes 1114144 | tf_op jit(solution)/shard_map/while/body/eval_jaxpr/ppermute | solution.py:26
  252.9 3.0 multiply_subtract_fusion.10
  261.0 4.0 %maximum_select_fusion.8 = f32[2,2,128,1024]{3,2,1,0:T(8,128)} fusion(f32[1,2,128,1024]{3,2,1,0:T(8,128)} %get-tuple-element.1320, f32[1,2,128,1024]{3,2,1,0:T(8,128)} %get-tuple-element.1321, f32[1,2,128,1024]{3,2,1,0:T(8,128)S(1)} %get-tuple-element.1322, f32[1,2,128,1024]{3,2,1,0:T(8,128)} %get-tuple-element.1323, ...), kind=kLoop, calls=%fused_computation.86.clone.1 | loop fusion | flops 2621440 | bytes 8388611 | tf_op jit(solution)/shard_map/while/body/eval_jaxpr/jit(_where)/select_n | solution.py:200
  265.0 10.5 %collective-permute-done.7 = bf16[2,2,128,1024]{3,2,1,0:T(8,128)(2,1)} collective-permute-done((bf16[2,2,128,1024]{3,2,1,0:T(8,128)(2,1)}, bf16[2,2,128,1024]{3,2,1,0:T(8,128)(2,1)}, u32[]{:S(2)}, u32[]{:S(2)}) %collective-permute-start.7) | collective-permute-done | bytes 1048608 | tf_op jit(solution)/shard_map/while/body/eval_jaxpr/ppermute | solution.py:26
  302.6 13.2 %collective-permute-done.6 = bf16[2,2,136,1024]{3,2,1,0:T(8,128)(2,1)S(1)} collective-permute-done((bf16[2,2,136,1024]{3,2,1,0:T(8,128)(2,1)S(1)}, bf16[2,2,136,1024]{3,2,1,0:T(8,128)(2,1)S(1)}, u32[]{:S(2)}, u32[]{:S(2)}) %collective-permute-start.6) | collective-permute-done | bytes 1114144 | tf_op jit(solution)/shard_map/while/body/eval_jaxpr/ppermute | solution.py:26
  332.5 3.0 multiply_subtract_fusion.10
  340.6 4.7 %maximum_select_fusion.8 = f32[2,2,128,1024]{3,2,1,0:T(8,128)} fusion(f32[1,2,128,1024]{3,2,1,0:T(8,128)} %get-tuple-element.1320, f32[1,2,128,1024]{3,2,1,0:T(8,128)} %get-tuple-element.1321, f32[1,2,128,1024]{3,2,1,0:T(8,128)S(1)} %get-tuple-element.1322, f32[1,2,128,1024]{3,2,1,0:T(8,128)} %get-tuple-element.1323, ...), kind=kLoop, calls=%fused_computation.86.clone.1 | loop fusion | flops 2621440 | bytes 8388611 | tf_op jit(solution)/shard_map/while/body/eval_jaxpr/jit(_where)/select_n | solution.py:200
  345.3 9.8 %collective-permute-done.7 = bf16[2,2,128,1024]{3,2,1,0:T(8,128)(2,1)} collective-permute-done((bf16[2,2,128,1024]{3,2,1,0:T(8,128)(2,1)}, bf16[2,2,128,1024]{3,2,1,0:T(8,128)(2,1)}, u32[]{:S(2)}, u32[]{:S(2)}) %collective-permute-start.7) | collective-permute-done | bytes 1048608 | tf_op jit(solution)/shard_map/while/body/eval_jaxpr/ppermute | solution.py:26
  357.7 25.6 %while.52 = (s32[]{:T(128)}, f32[2,2,128,2048]{3,2,1,0:T(8,128)}, s32[2]{0:T(128)S(1)}, s32[2]{0:T(128)S(1)}, f32[2,2,128,1024]{3,2,1,0:T(8,128)S(1)}, /*index=5*/s32[]{:T(128)}, s32[]{:T(128)}, s32[]{:T(128)}, s32[]{:T(128)}) while((s32[]{:T(128)}, f32[2,2,128,2048]{3,2,1,0:T(8,128)}, s32[2]{0:T(128)S(1)}, s32[2]{0:T(128)S(1)}, ...), condition=%wide.region_13.14_spmd, body=%wide.region_12.13_spmd.sunk | while | flops 262152 | bytes 5243081 | solution.py:215
  364.3 6.2 %dynamic_update_slice.8 = f32[2,2,128,2048]{3,2,1,0:T(8,128)} dynamic-update-slice(f32[2,2,128,2048]{3,2,1,0:T(8,128)} %get-tuple-element.1454, f32[2,1,128,1024]{3,2,1,0:T(8,128)S(1)} %dynamic-slice_add_fusion.2, s32[]{:T(128)} %constant.203.clone.1..sunk, s32[]{:T(128)S(6)} %select_n.337, s32[]{:T(128)} %constant.203.clone.1..sunk, s32[]{:T(128)S(6)} %select_n.338) | dynamic-update-slice | bytes 2097156 | tf_op jit(solution)/shard_map/while/body/eval_jaxpr/dynamic_update_slice | solution.py:213
  377.2 6.1 %dynamic_update_slice.8 = f32[2,2,128,2048]{3,2,1,0:T(8,128)} dynamic-update-slice(f32[2,2,128,2048]{3,2,1,0:T(8,128)} %get-tuple-element.1454, f32[2,1,128,1024]{3,2,1,0:T(8,128)S(1)} %dynamic-slice_add_fusion.2, s32[]{:T(128)} %constant.203.clone.1..sunk, s32[]{:T(128)S(6)} %select_n.337, s32[]{:T(128)} %constant.203.clone.1..sunk, s32[]{:T(128)S(6)} %select_n.338) | dynamic-update-slice | bytes 2097156 | tf_op jit(solution)/shard_map/while/body/eval_jaxpr/dynamic_update_slice | solution.py:213
  (263 shorter events, 195.4 us)
Async XLA Ops:
  0.0 7.1 %copy-start.14 = (bf16[2,9]{1,0:T(2,128)(2,1)S(1)}, bf16[2,9]{1,0:T(2,128)(2,1)}, u32[]{:S(2)}) copy-start(bf16[2,9]{1,0:T(2,128)(2,1)} %param.15) | copy-start | bytes 112
  0.0 8.8 %copy-start.13 = (s32[2,2]{1,0:T(2,128)S(1)}, s32[2,2]{1,0:T(2,128)}, u32[]{:S(2)}) copy-start(s32[2,2]{1,0:T(2,128)} %param.14) | copy-start | bytes 52
  0.0 11.9 %copy-start.9 = (f32[2,2,128,1024]{3,2,1,0:T(8,128)S(1)}, f32[2,2,128,1024]{3,2,1,0:T(8,128)}, u32[]{:S(2)}) copy-start(f32[2,2,128,1024]{3,2,1,0:T(8,128)} %param.12) | copy-start | bytes 6291460
  1.9 12.9 %collective-permute-start.8 = (f32[2,2,8,2048]{3,2,1,0:T(8,128)}, f32[2,2,8,2048]{3,2,1,0:T(8,128)S(1)}, u32[]{:S(2)}, u32[]{:S(2)}) collective-permute-start(f32[2,2,8,2048]{3,2,1,0:T(8,128)} %get-tuple-element.995), channel_id=1, source_target_pairs={{0,1},{1,2},{2,3},{3,4},{4,5},{5,6},{6,7},{7,0},{8,9},{9,10},{10,1... | collective-permute-start | bytes 786440 | tf_op jit(solution)/shard_map/ppermute | solution.py:14
  4.0 12.5 %collective-permute-start.9 = (f32[2,2,8,2048]{3,2,1,0:T(8,128)S(1)}, f32[2,2,8,2048]{3,2,1,0:T(8,128)S(1)}, u32[]{:S(2)}, u32[]{:S(2)}) collective-permute-start(f32[2,2,8,2048]{3,2,1,0:T(8,128)S(1)} %get-tuple-element.996), channel_id=1, source_target_pairs={{1,0},{2,1},{3,2},{4,3},{5,4},{6,5},{7,6},{0,7},{9,8},{10,9},{11,1... | collective-permute-start | bytes 786440 | tf_op jit(solution)/shard_map/ppermute | solution.py:16
  42.6 5.0 %collective-permute-start = (bf16[2,2,8,1024]{3,2,1,0:T(8,128)(2,1)S(1)}, bf16[2,2,8,1024]{3,2,1,0:T(8,128)(2,1)S(1)}, u32[]{:S(2)}, u32[]{:S(2)}) collective-permute-start(bf16[2,2,8,1024]{3,2,1,0:T(8,128)(2,1)S(1)} %get-tuple-element.1265), channel_id=1, source_target_pairs={{1,0},{2,1},{3,2},{4,3},{5,4},{6,5},{7,6},{0,7},{9,8},{10,9},{11,1... | collective-permute-start | bytes 196616 | tf_op jit(solution)/shard_map/while/body/eval_jaxpr/ppermute | solution.py:16
  46.3 6.1 %copy-start.6 = (f32[2,144,1024]{2,1,0:T(8,128)S(1)}, f32[2,144,1024]{2,1,0:T(8,128)}, u32[]{:S(2)}) copy-start(f32[2,144,1024]{2,1,0:T(8,128)} %get-tuple-element.1384) | copy-start | bytes 3538948 | tf_op jit(solution)/shard_map/while
  46.3 6.1 %copy-start.7 = (f32[2,144,1024]{2,1,0:T(8,128)S(1)}, f32[2,144,1024]{2,1,0:T(8,128)}, u32[]{:S(2)}) copy-start(f32[2,144,1024]{2,1,0:T(8,128)} %get-tuple-element.1381) | copy-start | bytes 3538948 | tf_op jit(solution)/shard_map/while
  46.3 5.8 %collective-permute-start.1 = (bf16[2,2,8,1024]{3,2,1,0:T(8,128)(2,1)S(1)}, bf16[2,2,8,1024]{3,2,1,0:T(8,128)(2,1)S(1)}, u32[]{:S(2)}, u32[]{:S(2)}) collective-permute-start(bf16[2,2,8,1024]{3,2,1,0:T(8,128)(2,1)S(1)} %get-tuple-element.1266), channel_id=1, source_target_pairs={{0,1},{1,2},{2,3},{3,4},{4,5},{5,6},{6,7},{7,0},{8,9},{9,10},{10,1... | collective-permute-start | bytes 196616 | tf_op jit(solution)/shard_map/while/body/eval_jaxpr/ppermute | solution.py:14
  66.3 18.7 %collective-permute-start.2 = (bf16[2,2,136,1024]{3,2,1,0:T(8,128)(2,1)}, bf16[2,2,136,1024]{3,2,1,0:T(8,128)(2,1)}, u32[]{:S(2)}, u32[]{:S(2)}) collective-permute-start(bf16[2,2,136,1024]{3,2,1,0:T(8,128)(2,1)} %pad_maximum_fusion.37), channel_id=1, source_target_pairs={{0,8},{8,16},{16,24},{1,9},{9,17},{17,25},{2,10},{10,18},{18,26},{... | collective-permute-start | bytes 3342344 | tf_op jit(solution)/shard_map/while/body/eval_jaxpr/ppermute | solution.py:26
  100.5 16.4 %collective-permute-start.3 = (bf16[2,2,128,1024]{3,2,1,0:T(8,128)(2,1)}, bf16[2,2,128,1024]{3,2,1,0:T(8,128)(2,1)}, u32[]{:S(2)}, u32[]{:S(2)}) collective-permute-start(bf16[2,2,128,1024]{3,2,1,0:T(8,128)(2,1)} %get-tuple-element.1283), channel_id=1, source_target_pairs={{0,8},{8,16},{16,24},{1,9},{9,17},{17,25},{2,10},{10,18},{18,26},{... | collective-permute-start | bytes 3145736 | tf_op jit(solution)/shard_map/while/body/eval_jaxpr/ppermute | solution.py:26
  118.2 3.2 collective-permute-start
  118.3 6.2 %copy-start.6 = (f32[2,144,1024]{2,1,0:T(8,128)S(1)}, f32[2,144,1024]{2,1,0:T(8,128)}, u32[]{:S(2)}) copy-start(f32[2,144,1024]{2,1,0:T(8,128)} %get-tuple-element.1384) | copy-start | bytes 3538948 | tf_op jit(solution)/shard_map/while
  118.3 6.2 %copy-start.7 = (f32[2,144,1024]{2,1,0:T(8,128)S(1)}, f32[2,144,1024]{2,1,0:T(8,128)}, u32[]{:S(2)}) copy-start(f32[2,144,1024]{2,1,0:T(8,128)} %get-tuple-element.1381) | copy-start | bytes 3538948 | tf_op jit(solution)/shard_map/while
  118.3 5.9 %collective-permute-start.1 = (bf16[2,2,8,1024]{3,2,1,0:T(8,128)(2,1)S(1)}, bf16[2,2,8,1024]{3,2,1,0:T(8,128)(2,1)S(1)}, u32[]{:S(2)}, u32[]{:S(2)}) collective-permute-start(bf16[2,2,8,1024]{3,2,1,0:T(8,128)(2,1)S(1)} %get-tuple-element.1266), channel_id=1, source_target_pairs={{0,1},{1,2},{2,3},{3,4},{4,5},{5,6},{6,7},{7,0},{8,9},{9,10},{10,1... | collective-permute-start | bytes 196616 | tf_op jit(solution)/shard_map/while/body/eval_jaxpr/ppermute | solution.py:14
  138.4 18.3 %collective-permute-start.2 = (bf16[2,2,136,1024]{3,2,1,0:T(8,128)(2,1)}, bf16[2,2,136,1024]{3,2,1,0:T(8,128)(2,1)}, u32[]{:S(2)}, u32[]{:S(2)}) collective-permute-start(bf16[2,2,136,1024]{3,2,1,0:T(8,128)(2,1)} %pad_maximum_fusion.37), channel_id=1, source_target_pairs={{0,8},{8,16},{16,24},{1,9},{9,17},{17,25},{2,10},{10,18},{18,26},{... | collective-permute-start | bytes 3342344 | tf_op jit(solution)/shard_map/while/body/eval_jaxpr/ppermute | solution.py:26
  172.4 16.4 %collective-permute-start.3 = (bf16[2,2,128,1024]{3,2,1,0:T(8,128)(2,1)}, bf16[2,2,128,1024]{3,2,1,0:T(8,128)(2,1)}, u32[]{:S(2)}, u32[]{:S(2)}) collective-permute-start(bf16[2,2,128,1024]{3,2,1,0:T(8,128)(2,1)} %get-tuple-element.1283), channel_id=1, source_target_pairs={{0,8},{8,16},{16,24},{1,9},{9,17},{17,25},{2,10},{10,18},{18,26},{... | collective-permute-start | bytes 3145736 | tf_op jit(solution)/shard_map/while/body/eval_jaxpr/ppermute | solution.py:26
  195.4 3.2 collective-permute-start.4
  195.5 5.9 %collective-permute-start.5 = (bf16[2,2,8,1024]{3,2,1,0:T(8,128)(2,1)S(1)}, bf16[2,2,8,1024]{3,2,1,0:T(8,128)(2,1)S(1)}, u32[]{:S(2)}, u32[]{:S(2)}) collective-permute-start(bf16[2,2,8,1024]{3,2,1,0:T(8,128)(2,1)S(1)} %get-tuple-element.1299), channel_id=1, source_target_pairs={{0,1},{1,2},{2,3},{3,4},{4,5},{5,6},{6,7},{7,0},{8,9},{9,10},{10,1... | collective-permute-start | bytes 196616 | tf_op jit(solution)/shard_map/while/body/eval_jaxpr/ppermute | solution.py:14
  217.3 2.2 copy-start.4
  217.4 18.8 %collective-permute-start.6 = (bf16[2,2,136,1024]{3,2,1,0:T(8,128)(2,1)S(1)}, bf16[2,2,136,1024]{3,2,1,0:T(8,128)(2,1)S(1)}, u32[]{:S(2)}, u32[]{:S(2)}) collective-permute-start(bf16[2,2,136,1024]{3,2,1,0:T(8,128)(2,1)S(1)} %pad_maximum_fusion.43), channel_id=1, source_target_pairs={{8,0},{16,8},{24,16},{9,1},{17,9},{25,17},{10,2},{18,10},{26,18},{... | collective-permute-start | bytes 3342344 | tf_op jit(solution)/shard_map/while/body/eval_jaxpr/ppermute | solution.py:26
  250.8 2.2 copy-start.1
  259.1 16.4 %collective-permute-start.7 = (bf16[2,2,128,1024]{3,2,1,0:T(8,128)(2,1)}, bf16[2,2,128,1024]{3,2,1,0:T(8,128)(2,1)}, u32[]{:S(2)}, u32[]{:S(2)}) collective-permute-start(bf16[2,2,128,1024]{3,2,1,0:T(8,128)(2,1)} %pad_maximum_fusion.45), channel_id=1, source_target_pairs={{8,0},{16,8},{24,16},{9,1},{17,9},{25,17},{10,2},{18,10},{26,18},{... | collective-permute-start | bytes 3145736 | tf_op jit(solution)/shard_map/while/body/eval_jaxpr/ppermute | solution.py:26
  276.9 3.2 collective-permute-start.4
  277.0 5.9 %collective-permute-start.5 = (bf16[2,2,8,1024]{3,2,1,0:T(8,128)(2,1)S(1)}, bf16[2,2,8,1024]{3,2,1,0:T(8,128)(2,1)S(1)}, u32[]{:S(2)}, u32[]{:S(2)}) collective-permute-start(bf16[2,2,8,1024]{3,2,1,0:T(8,128)(2,1)S(1)} %get-tuple-element.1299), channel_id=1, source_target_pairs={{0,1},{1,2},{2,3},{3,4},{4,5},{5,6},{6,7},{7,0},{8,9},{9,10},{10,1... | collective-permute-start | bytes 196616 | tf_op jit(solution)/shard_map/while/body/eval_jaxpr/ppermute | solution.py:14
  298.8 2.2 copy-start.4
  298.9 17.0 %collective-permute-start.6 = (bf16[2,2,136,1024]{3,2,1,0:T(8,128)(2,1)S(1)}, bf16[2,2,136,1024]{3,2,1,0:T(8,128)(2,1)S(1)}, u32[]{:S(2)}, u32[]{:S(2)}) collective-permute-start(bf16[2,2,136,1024]{3,2,1,0:T(8,128)(2,1)S(1)} %pad_maximum_fusion.43), channel_id=1, source_target_pairs={{8,0},{16,8},{24,16},{9,1},{17,9},{25,17},{10,2},{18,10},{26,18},{... | collective-permute-start | bytes 3342344 | tf_op jit(solution)/shard_map/while/body/eval_jaxpr/ppermute | solution.py:26
  330.4 2.2 copy-start.1
  338.7 16.4 %collective-permute-start.7 = (bf16[2,2,128,1024]{3,2,1,0:T(8,128)(2,1)}, bf16[2,2,128,1024]{3,2,1,0:T(8,128)(2,1)}, u32[]{:S(2)}, u32[]{:S(2)}) collective-permute-start(bf16[2,2,128,1024]{3,2,1,0:T(8,128)(2,1)} %pad_maximum_fusion.45), channel_id=1, source_target_pairs={{8,0},{16,8},{24,16},{9,1},{17,9},{25,17},{10,2},{18,10},{26,18},{... | collective-permute-start | bytes 3145736 | tf_op jit(solution)/shard_map/while/body/eval_jaxpr/ppermute | solution.py:26
  355.1 2.5 copy-start.3
  355.1 2.5 copy-start.15
  355.1 2.5 copy-start.16
  (12 other events, 15.2 us)
where the time goes:
time: 386 us; the launch traced here: 383 us
  waiting for transfers between devices  113 us (29%)
  other arithmetic  94.7 us (25%)
  local copies, waits for them, and re-layouts  89.5 us (23%)
  starting transfers between devices  41.4 us (11%)
  matrix products  35.6 us (9%)
  loops' own time  8.68 us (2%)
    ppermute x8, waiting for transfers between devices, from_behind(): return lax.ppermute(array, axis, pairs)  92.5 us
    another operation x20, local copies, waits for them, and re-layouts, along_cols(): joined = jnp.stack([direct[0] - crossed[1], crossed[0] + direct[1]])  33.5 us
    ppermute x8, starting transfers between devices, from_behind(): return lax.ppermute(array, axis, pairs)  28.2 us
    while x52, local copies, waits for them, and re-layouts  14.4 us
    another operation x18, other arithmetic  14.3 us
    ppermute x5, waiting for transfers between devices, with_halo(): lax.ppermute(tail, axis, [(i, (i + 1) % count) for i in range(count)])  13 us
    dynamic_update_slice x2, local copies, waits for them, and re-layouts, accumulate(): return lax.dynamic_update_slice(running, current + portion[:, None], corner)  12.3 us
    dot_general x8, matrix products, along_rows(): jnp.einsum('rq,xpqc->xprc', imag_mat, field_in, preferred_element_type=jn...  10.2 us
  transfers between devices with their start and end apart: 18, of which 18 were waited for; matrix products, arithmetic and copies ran while one was open for 7% of the time, Pallas kernels for 0%

commit v1 on v0

--- a/solution.py
+++ b/solution.py
@@ -1,6 +1,10 @@
+import functools
+
 import jax
 import jax.numpy as jnp
 from jax import lax
+from jax.experimental import pallas as pl
+from jax.experimental.pallas import tpu as pltpu
 from jax.sharding import PartitionSpec as P
 
 
@@ -216,13 +220,293 @@
     return gradient[:, None]
 
 
+ROW_BLOCK = 32
+
+
+def fits(mesh, potential_shape, incident_shape, kernel_shape):
+    depth_count, lat_count = mesh.shape["depth"], mesh.shape["lat"]
+    slices, window, columns = potential_shape[1], incident_shape[3], potential_shape[4]
+    half_width = (kernel_shape[1] - 1) // 2
+    if incident_shape[1] != 2 or depth_count != 4 or slices != 4:
+        return False
+    half_band = potential_shape[3] // lat_count // 2
+    reach = 2 * slices * half_width
+    return (
+        half_width <= 8
+        and reach <= half_band
+        and reach % 16 == 0
+        and half_band % ROW_BLOCK == 0
+        and (half_band + 2 * reach) % 128 == 0
+        and window % 128 == 0
+        and columns == 2 * window
+    )
+
+
+def transmission_kernel(scalars, pot_ref, out_ref):
+    col = scalars[2 + pl.program_id(0)]
+    columns, window = pot_ref.shape[3], out_ref.shape[3]
+    shift = lax.rem(columns - col, columns)
+    phase = pltpu.roll(pot_ref[0, 0], shift, 1)[:, :window]
+    absorb = pltpu.roll(pot_ref[1, 0], shift, 1)[:, :window]
+    damping = jnp.exp(-absorb)
+    out_ref[0, 0] = (damping * jnp.cos(phase)).astype(out_ref.dtype)
+    out_ref[0, 1] = (damping * jnp.sin(phase)).astype(out_ref.dtype)
+
+
+def transmissions(scalars, layer_pot, window):
+    band_rows, columns = layer_pot.shape[2:]
+    return pl.pallas_call(
+        transmission_kernel,
+        out_shape=jax.ShapeDtypeStruct((2, 2, band_rows, window), jnp.bfloat16),
+        grid_spec=pltpu.PrefetchScalarGridSpec(
+            num_scalar_prefetch=1,
+            grid=(2, band_rows // ROW_BLOCK),
+            in_specs=[
+                pl.BlockSpec((2, 1, ROW_BLOCK, columns), lambda q, r, sc: (0, sc[q], r, 0))
+            ],
+            out_specs=pl.BlockSpec((1, 2, ROW_BLOCK, window), lambda q, r, sc: (q, 0, r, 0)),
+        ),
+    )(scalars, layer_pot)
+
+
+def band(taps, rows, cols, start, half_width):
+    offset = (
+        lax.broadcasted_iota(jnp.int32, (rows, cols), 0)
+        - lax.broadcasted_iota(jnp.int32, (rows, cols), 1)
+        - start
+        + half_width
+    )
+    total = jnp.zeros((rows, cols), jnp.float32)
+    for tap_index, tap in enumerate(taps):
+        total = jnp.where(offset == tap_index, tap, total)
+    return total
+
+
+def main_kernel(sc, taps_ref, keep, recv, wave_ref, meas_ref, out_ref, waves, row_mat, col_mat):
+    rows, window = meas_ref.shape
+    slices = waves.shape[0]
+    tap_count = taps_ref.shape[1]
+    half_width = (tap_count - 1) // 2
+    reach = 2 * slices * half_width
+    base, half, probe = sc[0], sc[1], sc[2]
+    blocks = window // 128
+    re = [taps_ref[0, i] for i in range(tap_count)]
+    im = [taps_ref[1, i] for i in range(tap_count)]
+    ways = ((re, im), (re[::-1], [-tap for tap in im[::-1]]))
+    for way, (tap_re, tap_im) in enumerate(ways):
+        real = band(tap_re[::-1], rows, rows, 0, half_width)
+        imag = band(tap_im[::-1], rows, rows, 0, half_width)
+        row_mat[way, :rows, :rows] = real.astype(jnp.bfloat16)
+        row_mat[way, :rows, rows:] = (-imag).astype(jnp.bfloat16)
+        row_mat[way, rows:, :rows] = imag.astype(jnp.bfloat16)
+        row_mat[way, rows:, rows:] = real.astype(jnp.bfloat16)
+        real = band(tap_re, 384, 128, 128, half_width)
+        imag = band(tap_im, 384, 128, 128, half_width)
+        col_mat[way, :384, :128] = real.astype(jnp.bfloat16)
+        col_mat[way, :384, 128:] = imag.astype(jnp.bfloat16)
+        col_mat[way, 384:, :128] = (-imag).astype(jnp.bfloat16)
+        col_mat[way, 384:, 128:] = real.astype(jnp.bfloat16)
+
+    def rows_conv(field, way):
+        return jnp.dot(row_mat[way], field, preferred_element_type=jnp.float32).astype(
+            jnp.bfloat16
+        )
+
+    def cols_conv(field, way):
+        edge = jnp.zeros((rows, 128), jnp.bfloat16)
+        padded = [
+            jnp.concatenate([edge, field[k * rows : (k + 1) * rows], edge], axis=1)
+            for k in range(2)
+        ]
+        slabs = jnp.concatenate(
+            [
+                jnp.concatenate([part[:, 128 * b : 128 * b + 384] for part in padded], axis=1)
+                for b in range(blocks)
+            ],
+            axis=0,
+        )
+        out = jnp.dot(slabs, col_mat[way], preferred_element_type=jnp.float32)
+        out = out.astype(jnp.bfloat16)
+        return [
+            jnp.concatenate(
+                [out[b * rows : (b + 1) * rows, 128 * k : 128 * k + 128] for b in range(blocks)],
+                axis=1,
+            )
+            for k in range(2)
+        ]
+
+    def factor(s):
+        core, side = lax.rem(s + half, 2), lax.rem(s // 2 + probe, 2)
+        return [
+            jnp.where(core == 0, keep[side, k], recv[side, k]).astype(jnp.float32)
+            for k in range(2)
+        ]
+
+    wave = [wave_ref[0], wave_ref[1]]
+    for s in range(slices):
+        waves[s, 0], waves[s, 1] = wave
+        t_re, t_im = factor(s)
+        w_re, w_im = [part.astype(jnp.float32) for part in wave]
+        product = jnp.concatenate([t_re * w_re - t_im * w_im, t_re * w_im + t_im * w_re], axis=0)
+        wave = cols_conv(rows_conv(product.astype(jnp.bfloat16), 0), 0)
+
+    w_re, w_im = [part.astype(jnp.float32) for part in wave]
+    window_row = base + lax.broadcasted_iota(jnp.int32, (rows, window), 0)
+    inside = (window_row >= 0) & (window_row < window)
+    residual = 2.0 * (w_re * w_re + w_im * w_im - meas_ref[...])
+    residual = jnp.where(inside, residual, 0.0)
+    adjoint = [(residual * w_re).astype(jnp.bfloat16), (residual * w_im).astype(jnp.bfloat16)]
+    for s in reversed(range(slices)):
+        spread = cols_conv(jnp.concatenate(adjoint, axis=0), 1)
+        grad = rows_conv(jnp.concatenate(spread, axis=0), 1).astype(jnp.float32)
+        g_re, g_im = grad[:rows], grad[rows:]
+        t_re, t_im = factor(s)
+        back_re = t_re * g_re + t_im * g_im
+        back_im = t_re * g_im - t_im * g_re
+        own = slice(reach, rows - reach)
+        e_re = waves[s, 0, own].astype(jnp.float32)
+        e_im = waves[s, 1, own].astype(jnp.float32)
+        core, side = lax.rem(s + half, 2), lax.rem(s // 2 + probe, 2)
+        out_ref[core, side, 0] = (e_re * back_im[own] - e_im * back_re[own]).astype(jnp.bfloat16)
+        out_ref[core, side, 1] = (-e_re * back_re[own] - e_im * back_im[own]).astype(jnp.bfloat16)
+        adjoint = [back_re.astype(jnp.bfloat16), back_im.astype(jnp.bfloat16)]
+
+
+def section_terms(scalars, taps, keep, recv, wave, meas, half_band):
+    slices, rows, window = 4, meas.shape[0], meas.shape[1]
+    smem = pl.BlockSpec(memory_space=pltpu.SMEM)
+    vmem = pl.BlockSpec(memory_space=pltpu.VMEM)
+    return pl.pallas_call(
+        main_kernel,
+        out_shape=jax.ShapeDtypeStruct((2, 2, 2, half_band, window), jnp.bfloat16),
+        in_specs=[smem, smem, vmem, vmem, vmem, vmem],
+        out_specs=vmem,
+        scratch_shapes=[
+            pltpu.VMEM((slices, 2, rows, window), jnp.bfloat16),
+            pltpu.VMEM((2, 2 * rows, 2 * rows), jnp.bfloat16),
+            pltpu.VMEM((2, 768, 256), jnp.bfloat16),
+        ],
+        compiler_params=pltpu.CompilerParams(vmem_limit_bytes=48 * 1024 * 1024),
+    )(scalars, taps, keep, recv, wave, meas)
+
+
+def place_kernel(scalars, own_ref, other_ref, out_ref):
+    columns, window = out_ref.shape[3], own_ref.shape[3]
+    for part in range(2):
+        totals = [None, None]
+        for q, ref in enumerate((own_ref, other_ref)):
+            values = ref[0, part].astype(jnp.float32)
+            wide = jnp.concatenate([values, jnp.zeros_like(values)], axis=1)
+            wide = pltpu.roll(wide, scalars[2 + q], 1)
+            for layer in range(2):
+                term = jnp.where(scalars[q] == layer, wide, 0.0)
+                totals[layer] = term if q == 0 else totals[layer] + term
+        for layer in range(2):
+            out_ref[part, layer] = totals[layer]
+
+
+def placed(scalars, own, other, columns):
+    half_band, window = own.shape[2:]
+    per_half = half_band // ROW_BLOCK
+
+    def pick(r, sc):
+        return (lax.rem(r // per_half + sc[4], 2), 0, lax.rem(r, per_half), 0)
+
+    spec = pl.BlockSpec((1, 2, ROW_BLOCK, window), pick)
+    return pl.pallas_call(
+        place_kernel,
+        out_shape=jax.ShapeDtypeStruct((2, 2, 2 * half_band, columns), jnp.float32),
+        grid_spec=pltpu.PrefetchScalarGridSpec(
+            num_scalar_prefetch=1,
+            grid=(2 * per_half,),
+            in_specs=[spec, spec],
+            out_specs=pl.BlockSpec((2, 2, ROW_BLOCK, columns), lambda r, sc: (0, 0, r, 0)),
+        ),
+    )(scalars, own, other)
+
+
+def local_fast(potential, incident, measured, offsets, kernel):
+    lat_count = lax.axis_size("lat")
+    lat_index = lax.axis_index("lat")
+    depth_index = lax.axis_index("depth")
+    band_rows, columns = potential.shape[3:]
+    window = incident.shape[3]
+    half_width = (kernel.shape[1] - 1) // 2
+    half_band = band_rows // 2
+    reach = 8 * half_width
+    rows = half_band + 2 * reach
+    probe, half = depth_index // 2, depth_index % 2
+    order = jnp.stack([probe, 1 - probe])
+    first_band = offsets[:, 0][order] // band_rows
+    place_band = (lat_index - first_band) % lat_count
+    own_layer = (first_band + place_band) // lat_count
+    scalars = jnp.concatenate([own_layer, offsets[:, 1][order], half[None]]).astype(jnp.int32)
+
+    own_t = transmissions(scalars, potential[:, 0], window)
+    up = [(i, (i + 1) % lat_count) for i in range(lat_count)]
+    down = [((i + 1) % lat_count, i) for i in range(lat_count)]
+    above = lax.ppermute(own_t[:, :, band_rows - reach :], "lat", up)
+    below = lax.ppermute(own_t[:, :, :reach], "lat", down)
+    none = jnp.zeros((), jnp.bfloat16)
+    above = jnp.where((place_band > 0)[:, None, None, None], above, none)
+    below = jnp.where((place_band < lat_count - 1)[:, None, None, None], below, none)
+    ext_t = jnp.concatenate([above, own_t, below], axis=2)
+
+    across = [(i, i ^ 2) for i in range(4)]
+    beside = [(i, i ^ 1) for i in range(4)]
+    far_t = lax.ppermute(ext_t[1], "depth", across)
+    both_t = jnp.stack([ext_t[0], far_t])
+    keep_t = lax.dynamic_slice_in_dim(both_t, half * half_band, rows, 2)
+    send_t = lax.dynamic_slice_in_dim(both_t, (1 - half) * half_band, rows, 2)
+    recv_t = lax.ppermute(send_t, "depth", beside)
+
+    ring = []
+    for d in range(4):
+        for i in range(lat_count):
+            to = (i + 1) % lat_count if d % 2 == 0 else (i - 1) % lat_count
+            ring.append((d * lat_count + i, d * lat_count + to))
+
+    def extended(array):
+        axis = array.ndim - 2
+        tail = lax.slice_in_dim(array, band_rows - reach, band_rows, axis=axis)
+        front = lax.slice_in_dim(array, 0, reach, axis=axis)
+        edge = lax.ppermute(jnp.where(half == 0, tail, front), ("depth", "lat"), ring)
+        kept = rows - reach
+        low = jnp.concatenate([edge, lax.slice_in_dim(array, 0, kept, axis=axis)], axis)
+        high = jnp.concatenate(
+            [lax.slice_in_dim(array, band_rows - kept, band_rows, axis=axis), edge], axis
+        )
+        return jnp.where(half == 0, low, high)
+
+    wave = extended(
+        lax.dynamic_index_in_dim(incident, probe, 1, keepdims=False).astype(jnp.bfloat16)
+    )
+    meas = extended(lax.dynamic_index_in_dim(measured, probe, 0, keepdims=False))
+
+    base = place_band[0] * band_rows + half * half_band - reach
+    facts = jnp.stack([base, half, probe]).astype(jnp.int32)
+    terms = section_terms(
+        facts, kernel.astype(jnp.float32), keep_t, recv_t, wave, meas, half_band
+    )
+    joined = jnp.stack([terms[0], lax.ppermute(terms[1], "depth", beside)], axis=1)
+    other = lax.ppermute(joined[1], "depth", across)
+    return placed(scalars, joined[0], other, columns)[:, None]
+
+
 def solution(mesh):
-    in_specs = (
-        P(None, "depth", None, "lat", None),
-        P(None, None, "lat", None),
-        P(None, "lat", None),
-        P(),
-        P(),
-    )
-    out_specs = P(None, "depth", None, "lat", None)
-    return jax.shard_map(local, mesh=mesh, in_specs=in_specs, out_specs=out_specs, check_vma=False)
+    def run(*args):
+        potential, incident, _, _, kernel = args
+        body = local_fast if fits(mesh, potential.shape, incident.shape, kernel.shape) else local
+        in_specs = (
+            P(None, "depth", None, "lat", None),
+            P(None, None, "lat", None),
+            P(None, "lat", None),
+            P(),
+            P(),
+        )
+        out_specs = P(None, "depth", None, "lat", None)
+        return jax.shard_map(
+            body, mesh=mesh, in_specs=in_specs, out_specs=out_specs, check_vma=False
+        )(*args)
+
+    return run

time: 386 us -> 99.7 us (0.26)
  the two profiles are of different devices: /device:TPU:1 before, /device:TPU:0 now
where the time goes in v1:
time: 99.7 us; the launch traced here: 99.1 us
  waiting for transfers between devices  43.4 us (44%)
  Pallas kernels  25.2 us (25%)
  local copies, waits for them, and re-layouts  10.4 us (10%)
  starting transfers between devices  10.3 us (10%)
  other arithmetic  9.59 us (10%)
    ppermute x1, waiting for transfers between devices, local_fast(): far_t = lax.ppermute(ext_t[1], 'depth', across)  14.8 us
    ppermute x1, waiting for transfers between devices, local_fast(): other = lax.ppermute(joined[1], 'depth', across)  12.4 us
    pallas_call x1, Pallas kernels, section_terms(): pl.pallas_call(main_kernel, out_shape=jax.ShapeDtypeStruct((2, 2, 2, half...  10.2 us
    pallas_call x1, Pallas kernels, transmissions(): pl.pallas_call(transmission_kernel, out_shape=jax.ShapeDtypeStruct((2, 2,...  9.59 us
    ppermute x1, waiting for transfers between devices, local_fast(): above = lax.ppermute(own_t[:, :, band_rows - reach:], 'lat', up)  8.07 us
    pallas_call x1, Pallas kernels, placed(): pl.pallas_call(place_kernel, out_shape=jax.ShapeDtypeStruct((2, 2, 2 * ha...  5.38 us
    ppermute x2, waiting for transfers between devices, extended(): lax.ppermute(jnp.where(half == 0, tail, front), ('depth', 'lat'), ring)  4.15 us
    ppermute x1, starting transfers between devices, local_fast(): below = lax.ppermute(own_t[:, :, :reach], 'lat', down)  3.1 us
  transfers between devices with their start and end apart: 8, of which 6 were waited for; matrix products, arithmetic and copies ran while one was open for 11% of the time, Pallas kernels for 0%

profile of v1, /device:TPU:0, one launch (start us, length us, event | category | flops | bytes accessed | tf_op | source)
XLA Modules:
  0.0 99.1 jit_solution(484020073861174007)
XLA Ops:
  0.0 1.1 %slice_reduce_fusion.1 = (s32[2]{0:T(128)S(1)}, s32[2]{0:T(128)S(1)}) fusion(s32[2,2]{1,0:T(2,128)} %param.8), kind=kLoop, calls=%fused_computation.43 | loop fusion | bytes 32 | tf_op jit(solution)/shard_map/slice | solution.py:440
  1.1 0.6 gather_fusion.1
  1.8 0.6 gather_fusion
  2.5 0.6 pad_add_fusion.scalars
  3.1 9.6 %shard_map.55 = bf16[2,2,128,1024]{3,2,1,0:T(8,128)(2,1)} custom-call(s32[5]{0:T(128)} %pad_add_fusion.scalars, f32[2,2,128,2048]{3,2,1,0:T(8,128)} %bitcast.37), custom_call_target="tpu_custom_call" | custom-call | tf_op jit(solution)/shard_map/pallas_call | solution.py:258
  12.7 1.2 %fusion.9 = (bf16[2,2,32,1024]{3,2,1,0:T(8,128)(2,1)S(1)}, bf16[2,2,32,1024]{3,2,1,0:T(8,128)(2,1)S(1)}) fusion(bf16[2,2,128,1024]{3,2,1,0:T(8,128)(2,1)} %shard_map.55), kind=kLoop, calls=%fused_computation.50 | loop fusion | bytes 1048576 | tf_op jit(solution)/shard_map/slice | solution.py:448
  13.8 3.0 %collective-permute-start = (bf16[2,2,32,1024]{3,2,1,0:T(8,128)(2,1)S(1)}, bf16[2,2,32,1024]{3,2,1,0:T(8,128)(2,1)S(1)}, u32[]{:S(2)}, u32[]{:S(2)}) collective-permute-start(bf16[2,2,32,1024]{3,2,1,0:T(8,128)(2,1)S(1)} %get-tuple-element.20), channel_id=1, source_target_pairs={{0,1},{1,2},{2,3},{3,4},{4,5},{5,6},{6,7},{7,0},{8,9},{9,10},{10,1... | collective-permute-start | bytes 786440 | tf_op jit(solution)/shard_map/ppermute | solution.py:448
  16.8 3.1 %collective-permute-start.1 = (bf16[2,2,32,1024]{3,2,1,0:T(8,128)(2,1)S(1)}, bf16[2,2,32,1024]{3,2,1,0:T(8,128)(2,1)S(1)}, u32[]{:S(2)}, u32[]{:S(2)}) collective-permute-start(bf16[2,2,32,1024]{3,2,1,0:T(8,128)(2,1)S(1)} %get-tuple-element.21), channel_id=1, source_target_pairs={{1,0},{2,1},{3,2},{4,3},{5,4},{6,5},{7,6},{0,7},{9,8},{10,9},{11,1... | collective-permute-start | bytes 786440 | tf_op jit(solution)/shard_map/ppermute | solution.py:449
  19.9 8.1 %collective-permute-done = bf16[2,2,32,1024]{3,2,1,0:T(8,128)(2,1)S(1)} collective-permute-done((bf16[2,2,32,1024]{3,2,1,0:T(8,128)(2,1)S(1)}, bf16[2,2,32,1024]{3,2,1,0:T(8,128)(2,1)S(1)}, u32[]{:S(2)}, u32[]{:S(2)}) %collective-permute-start) | collective-permute-done | bytes 262176 | tf_op jit(solution)/shard_map/ppermute | solution.py:448
  28.1 2.1 %collective-permute-done.1 = bf16[2,2,32,1024]{3,2,1,0:T(8,128)(2,1)S(1)} collective-permute-done((bf16[2,2,32,1024]{3,2,1,0:T(8,128)(2,1)S(1)}, bf16[2,2,32,1024]{3,2,1,0:T(8,128)(2,1)S(1)}, u32[]{:S(2)}, u32[]{:S(2)}) %collective-permute-start.1) | collective-permute-done | bytes 262176 | tf_op jit(solution)/shard_map/ppermute | solution.py:449
  30.4 1.3 %slice_bitcast_fusion = (bf16[2,192,1024]{2,1,0:T(8,128)(2,1)}, bf16[1,2,192,1024]{3,2,1,0:T(8,128)(2,1)}) fusion(bf16[2,2,192,1024]{3,2,1,0:T(8,128)(2,1)S(1)} %pad_maximum_fusion), kind=kLoop, calls=%fused_computation.12 | loop fusion | bytes 3145728 | tf_op jit(solution)/shard_map/squeeze | solution.py:457
  31.7 1.5 %collective-permute-start.2 = (bf16[2,192,1024]{2,1,0:T(8,128)(2,1)}, bf16[2,192,1024]{2,1,0:T(8,128)(2,1)S(1)}, u32[]{:S(2)}, u32[]{:S(2)}) collective-permute-start(bf16[2,192,1024]{2,1,0:T(8,128)(2,1)} %get-tuple-element.12), channel_id=1, source_target_pairs={{0,16},{8,24},{16,0},{24,8},{1,17},{9,25},{17,1},{25,9},{2,18},{10... | collective-permute-start | bytes 2359304 | tf_op jit(solution)/shard_map/ppermute | solution.py:457
  33.2 1.6 %fusion.6 = f32[32,1024]{1,0:T(8,128)} fusion(f32[2,128,1024]{2,1,0:T(8,128)} %param.7, s32[]{:T(128)S(6)} %select_n.116, s32[]{:T(128)S(6)} %add.72, pred[]{:T(512)S(6)} %eq.6), kind=kLoop, calls=%fused_computation.27 | loop fusion | flops 32768 | bytes 393225 | tf_op jit(solution)/shard_map/jit(_where)/select_n | solution.py:473
  34.9 0.4 collective-permute-start.5
  35.2 14.8 %collective-permute-done.2 = bf16[2,192,1024]{2,1,0:T(8,128)(2,1)S(1)} collective-permute-done((bf16[2,192,1024]{2,1,0:T(8,128)(2,1)}, bf16[2,192,1024]{2,1,0:T(8,128)(2,1)S(1)}, u32[]{:S(2)}, u32[]{:S(2)}) %collective-permute-start.2) | collective-permute-done | bytes 786464 | tf_op jit(solution)/shard_map/ppermute | solution.py:457
  50.0 0.9 copy-done.4
  50.9 2.7 %fusion = (bf16[2,2,128,1024]{3,2,1,0:T(8,128)(2,1)}, bf16[2,2,128,1024]{3,2,1,0:T(8,128)(2,1)S(1)}) fusion(s32[]{:T(128)S(6)} %select_n.113, bf16[1,2,192,1024]{3,2,1,0:T(8,128)(2,1)} %get-tuple-element.13, bf16[1,2,192,1024]{3,2,1,0:T(8,128)(2,1)} %bitcast.38, s32[]{:T(128)S(6)} %select_n.112), kind=kLoop, calls=%fused_computation.7 | loop fusion | flops 4194304 | bytes 3670024 | tf_op jit(solution)/shard_map/stack | solution.py:458
  53.7 0.8 copy-done.2
  54.6 0.7 slice_select_fusion
  55.2 0.7 collective-permute-start.4
  55.9 2.1 %fusion.10 = (bf16[2,96,1024]{2,1,0:T(8,128)(2,1)}, bf16[2,96,1024]{2,1,0:T(8,128)(2,1)}) fusion(bf16[2,128,1024]{2,1,0:T(8,128)(2,1)} %copy-done.2), kind=kLoop, calls=%fused_computation.51 | loop fusion | bytes 1572864 | tf_op jit(solution)/shard_map/slice | solution.py:477
  58.1 0.8 dynamic-slice_bitcast_fusion
  59.0 4.2 %collective-permute-done.4 = bf16[2,32,1024]{2,1,0:T(8,128)(2,1)} collective-permute-done((bf16[2,32,1024]{2,1,0:T(8,128)(2,1)}, bf16[2,32,1024]{2,1,0:T(8,128)(2,1)}, u32[]{:S(2)}, u32[]{:S(2)}) %collective-permute-start.4) | collective-permute-done | bytes 131104 | tf_op jit(solution)/shard_map/ppermute | solution.py:473
  63.2 1.4 %maximum_select_fusion.wave_ref = bf16[2,128,1024]{2,1,0:T(8,128)(2,1)S(1)} fusion(bf16[2,96,1024]{2,1,0:T(8,128)(2,1)} %get-tuple-element.23, bf16[2,32,1024]{2,1,0:T(8,128)(2,1)} %collective-permute-done.4, bf16[2,96,1024]{2,1,0:T(8,128)(2,1)} %get-tuple-element.22, pred[]{:T(512)S(6)} %eq.6), kind=kLoop, calls=%fused_computation.20 | loop fusion | flops 2359296 | bytes 1441793 | tf_op jit(solution)/shard_map/jit(_where)/select_n | solution.py:479
  64.6 1.1 %maximum_select_fusion.1.meas_ref = f32[128,1024]{1,0:T(8,128)S(1)} fusion(f32[96,1024]{1,0:T(8,128)} %get-tuple-element.19, f32[32,1024]{1,0:T(8,128)} %collective-permute-done.5, f32[96,1024]{1,0:T(8,128)S(1)} %get-tuple-element.18, pred[]{:T(512)S(6)} %eq.6), kind=kLoop, calls=%fused_computation.21 | loop fusion | flops 393216 | bytes 1441793 | tf_op jit(solution)/shard_map/jit(_where)/select_n | solution.py:479
  65.8 10.2 %shard_map.56 = bf16[2,2,2,64,1024]{4,3,2,1,0:T(8,128)(2,1)S(1)} custom-call(s32[3]{0:T(128)S(1)} %pad_add_fusion.1.sc, f32[2,9]{1,0:T(2,128)S(1)} %convert_element_type.9.taps_ref, bf16[2,2,128,1024]{3,2,1,0:T(8,128)(2,1)S(1)} %get-tuple-element.11.keep, bf16[2,2,128,1024]{3,2,1,0:T(8,128)(2,1)} %collective-permute-done.3.recv, ...), custom_call_target="tpu_custom_call" | custom-call | tf_op jit(solution)/shard_map/pallas_call | solution.py:379
  76.2 1.9 %collective-permute-done.6 = bf16[2,2,64,1024]{3,2,1,0:T(8,128)(2,1)S(1)} collective-permute-done((bf16[2,2,64,1024]{3,2,1,0:T(8,128)(2,1)S(1)}, bf16[2,2,64,1024]{3,2,1,0:T(8,128)(2,1)S(1)}, u32[]{:S(2)}, u32[]{:S(2)}) %collective-permute-start.6) | collective-permute-done | bytes 524320 | tf_op jit(solution)/shard_map/ppermute | solution.py:491
  78.1 0.9 fusion.5
  79.0 1.5 %collective-permute-start.7 = (bf16[2,2,64,1024]{3,2,1,0:T(8,128)(2,1)S(1)}, bf16[2,2,64,1024]{3,2,1,0:T(8,128)(2,1)S(1)}, u32[]{:S(2)}, u32[]{:S(2)}) collective-permute-start(bf16[2,2,64,1024]{3,2,1,0:T(8,128)(2,1)S(1)} %get-tuple-element.14), channel_id=1, source_target_pairs={{0,16},{8,24},{16,0},{24,8},{1,17},{9,25},{17,1},{25,9},{2,18},{10... | collective-permute-start | bytes 1572872 | tf_op jit(solution)/shard_map/ppermute | solution.py:492
  80.5 12.4 %collective-permute-done.7.other_ref = bf16[2,2,64,1024]{3,2,1,0:T(8,128)(2,1)S(1)} collective-permute-done((bf16[2,2,64,1024]{3,2,1,0:T(8,128)(2,1)S(1)}, bf16[2,2,64,1024]{3,2,1,0:T(8,128)(2,1)S(1)}, u32[]{:S(2)}, u32[]{:S(2)}) %collective-permute-start.7) | collective-permute-done | bytes 524320 | tf_op jit(solution)/shard_map/ppermute | solution.py:492
  93.0 0.8 copy-done.5
  93.8 5.4 %shard_map.57 = f32[2,2,128,2048]{3,2,1,0:T(8,128)} custom-call(s32[5]{0:T(128)} %pad_add_fusion.scalars, bf16[2,2,64,1024]{3,2,1,0:T(8,128)(2,1)} %get-tuple-element.15.own_ref, bf16[2,2,64,1024]{3,2,1,0:T(8,128)(2,1)} %copy-done.5), custom_call_target="tpu_custom_call" | custom-call | tf_op jit(solution)/shard_map/pallas_call | solution.py:416
  (27 shorter events, 0.8 us)
Async XLA Ops:
  0.0 53.6 %copy-start = (f32[2,2,128,1024]{3,2,1,0:T(8,128)S(1)}, f32[2,2,128,1024]{3,2,1,0:T(8,128)}, u32[]{:S(2)}) copy-start(f32[2,2,128,1024]{3,2,1,0:T(8,128)} %param.6) | copy-start | bytes 6291460
  12.7 17.6 %copy-start.1 = (bf16[2,2,128,1024]{3,2,1,0:T(8,128)(2,1)S(1)}, bf16[2,2,128,1024]{3,2,1,0:T(8,128)(2,1)}, u32[]{:S(2)}) copy-start(bf16[2,2,128,1024]{3,2,1,0:T(8,128)(2,1)} %shard_map.55) | copy-start | bytes 3145732
  13.8 14.2 %collective-permute-start = (bf16[2,2,32,1024]{3,2,1,0:T(8,128)(2,1)S(1)}, bf16[2,2,32,1024]{3,2,1,0:T(8,128)(2,1)S(1)}, u32[]{:S(2)}, u32[]{:S(2)}) collective-permute-start(bf16[2,2,32,1024]{3,2,1,0:T(8,128)(2,1)S(1)} %get-tuple-element.20), channel_id=1, source_target_pairs={{0,1},{1,2},{2,3},{3,4},{4,5},{5,6},{6,7},{7,0},{8,9},{9,10},{10,1... | collective-permute-start | bytes 786440 | tf_op jit(solution)/shard_map/ppermute | solution.py:448
  16.8 13.4 %collective-permute-start.1 = (bf16[2,2,32,1024]{3,2,1,0:T(8,128)(2,1)S(1)}, bf16[2,2,32,1024]{3,2,1,0:T(8,128)(2,1)S(1)}, u32[]{:S(2)}, u32[]{:S(2)}) collective-permute-start(bf16[2,2,32,1024]{3,2,1,0:T(8,128)(2,1)S(1)} %get-tuple-element.21), channel_id=1, source_target_pairs={{1,0},{2,1},{3,2},{4,3},{5,4},{6,5},{7,6},{0,7},{9,8},{10,9},{11,1... | collective-permute-start | bytes 786440 | tf_op jit(solution)/shard_map/ppermute | solution.py:449
  31.7 18.3 %collective-permute-start.2 = (bf16[2,192,1024]{2,1,0:T(8,128)(2,1)}, bf16[2,192,1024]{2,1,0:T(8,128)(2,1)S(1)}, u32[]{:S(2)}, u32[]{:S(2)}) collective-permute-start(bf16[2,192,1024]{2,1,0:T(8,128)(2,1)} %get-tuple-element.12), channel_id=1, source_target_pairs={{0,16},{8,24},{16,0},{24,8},{1,17},{9,25},{17,1},{25,9},{2,18},{10... | collective-permute-start | bytes 2359304 | tf_op jit(solution)/shard_map/ppermute | solution.py:457
  34.9 29.8 %collective-permute-start.5 = (f32[32,1024]{1,0:T(8,128)}, f32[32,1024]{1,0:T(8,128)}, u32[]{:S(2)}, u32[]{:S(2)}) collective-permute-start(f32[32,1024]{1,0:T(8,128)} %fusion.6), channel_id=1, source_target_pairs={{0,1},{1,2},{2,3},{3,4},{4,5},{5,6},{6,7},{7,0},{8,15},{9,8},{10,9... | collective-permute-start | bytes 393224 | tf_op jit(solution)/shard_map/ppermute | solution.py:473
  50.0 0.9 copy-start.4
  53.6 5.4 %copy-start.6 = (bf16[2,9]{1,0:T(2,128)(2,1)S(1)}, bf16[2,9]{1,0:T(2,128)(2,1)}, u32[]{:S(2)}) copy-start(bf16[2,9]{1,0:T(2,128)(2,1)} %param.9) | copy-start | bytes 112
  53.6 12.1 %collective-permute-start.3 = (bf16[2,2,128,1024]{3,2,1,0:T(8,128)(2,1)}, bf16[2,2,128,1024]{3,2,1,0:T(8,128)(2,1)}, u32[]{:S(2)}, u32[]{:S(2)}) collective-permute-start(bf16[2,2,128,1024]{3,2,1,0:T(8,128)(2,1)} %get-tuple-element.10), channel_id=1, source_target_pairs={{0,8},{8,0},{16,24},{24,16},{1,9},{9,1},{17,25},{25,17},{2,10},{10... | collective-permute-start | bytes 3145736 | tf_op jit(solution)/shard_map/ppermute | solution.py:461
  53.7 0.8 copy-start.2
  55.2 8.0 %collective-permute-start.4 = (bf16[2,32,1024]{2,1,0:T(8,128)(2,1)}, bf16[2,32,1024]{2,1,0:T(8,128)(2,1)}, u32[]{:S(2)}, u32[]{:S(2)}) collective-permute-start(bf16[2,32,1024]{2,1,0:T(8,128)(2,1)} %slice_select_fusion), channel_id=1, source_target_pairs={{0,1},{1,2},{2,3},{3,4},{4,5},{5,6},{6,7},{7,0},{8,15},{9,8},{10,9... | collective-permute-start | bytes 393224 | tf_op jit(solution)/shard_map/ppermute | solution.py:473
  55.9 2.1 %copy-start.3 = (f32[2,128,1024]{2,1,0:T(8,128)S(1)}, f32[2,128,1024]{2,1,0:T(8,128)}, u32[]{:S(2)}) copy-start(f32[2,128,1024]{2,1,0:T(8,128)} %param.7) | copy-start | bytes 3145732
  76.1 2.0 %collective-permute-start.6 = (bf16[2,2,64,1024]{3,2,1,0:T(8,128)(2,1)S(1)}, bf16[2,2,64,1024]{3,2,1,0:T(8,128)(2,1)S(1)}, u32[]{:S(2)}, u32[]{:S(2)}) collective-permute-start(bf16[2,2,64,1024]{3,2,1,0:T(8,128)(2,1)S(1)} %get-tuple-element.16), channel_id=1, source_target_pairs={{0,8},{8,0},{16,24},{24,16},{1,9},{9,1},{17,25},{25,17},{2,10},{10... | collective-permute-start | bytes 1572872 | tf_op jit(solution)/shard_map/ppermute | solution.py:491
  79.0 14.0 %collective-permute-start.7 = (bf16[2,2,64,1024]{3,2,1,0:T(8,128)(2,1)S(1)}, bf16[2,2,64,1024]{3,2,1,0:T(8,128)(2,1)S(1)}, u32[]{:S(2)}, u32[]{:S(2)}) collective-permute-start(bf16[2,2,64,1024]{3,2,1,0:T(8,128)(2,1)S(1)} %get-tuple-element.14), channel_id=1, source_target_pairs={{0,16},{8,24},{16,0},{24,8},{1,17},{9,25},{17,1},{25,9},{2,18},{10... | collective-permute-start | bytes 1572872 | tf_op jit(solution)/shard_map/ppermute | solution.py:492
  93.0 0.8 copy-start.5

commit v2 on v1

--- a/solution.py
+++ b/solution.py
@@ -230,16 +230,22 @@
     if incident_shape[1] != 2 or depth_count != 4 or slices != 4:
         return False
     half_band = potential_shape[3] // lat_count // 2
-    reach = 2 * slices * half_width
+    reach = slices * half_width
     return (
         half_width <= 8
-        and reach <= half_band
+        and 2 * reach <= half_band
         and reach % 16 == 0
         and half_band % ROW_BLOCK == 0
-        and (half_band + 2 * reach) % 128 == 0
         and window % 128 == 0
         and columns == 2 * window
     )
+
+
+def series(square, divisors):
+    total = 1.0 / divisors[-1]
+    for divisor in divisors[-2::-1]:
+        total = total * square + 1.0 / divisor
+    return total
 
 
 def transmission_kernel(scalars, pot_ref, out_ref):
@@ -249,8 +255,12 @@
     phase = pltpu.roll(pot_ref[0, 0], shift, 1)[:, :window]
     absorb = pltpu.roll(pot_ref[1, 0], shift, 1)[:, :window]
     damping = jnp.exp(-absorb)
-    out_ref[0, 0] = (damping * jnp.cos(phase)).astype(out_ref.dtype)
-    out_ref[0, 1] = (damping * jnp.sin(phase)).astype(out_ref.dtype)
+    turn = 0.5 * phase
+    square = turn * turn
+    sine = turn * series(square, (1, -6, 120, -5040, 362880, -39916800, 6227020800))
+    cosine = series(square, (1, -2, 24, -720, 40320, -3628800, 479001600))
+    out_ref[0, 0] = (damping * (1.0 - 2.0 * sine * sine)).astype(out_ref.dtype)
+    out_ref[0, 1] = (2.0 * damping * sine * cosine).astype(out_ref.dtype)
 
 
 def transmissions(scalars, layer_pot, window):
@@ -282,24 +292,110 @@
     return total
 
 
-def main_kernel(sc, taps_ref, keep, recv, wave_ref, meas_ref, out_ref, waves, row_mat, col_mat):
-    rows, window = meas_ref.shape
-    slices = waves.shape[0]
+def main_kernel(
+    flags, taps_ref, own_t, incident, measured, out_ref,
+    t_all, start, waves, adj, terms, row_mat, col_mat,
+    send_sem, far_sem, beside_sem, edge_sem, start_sem, adj_sem, term_sem,
+):
+    slices, _, rows, window = waves.shape
     tap_count = taps_ref.shape[1]
     half_width = (tap_count - 1) // 2
-    reach = 2 * slices * half_width
-    base, half, probe = sc[0], sc[1], sc[2]
+    band_rows = own_t.shape[2]
+    half_band = band_rows // 2
+    reach = (rows - half_band) // 2
     blocks = window // 128
+    depth, lat = lax.axis_index("depth"), lax.axis_index("lat")
+    lat_count = lax.axis_size("lat")
+    probe, half = depth // 2, lax.rem(depth, 2)
+    other_half = 1 - half
+    beside = 2 * probe + other_half
+    across = 2 * (1 - probe) + half
+    before, after = lax.rem(lat + lat_count - 1, lat_count), lax.rem(lat + 1, lat_count)
+    near = lax.rem(lat + 2 * half + lat_count - 1, lat_count)
+
+    def remote(src, dst, send, recv, to):
+        return pltpu.make_async_remote_copy(
+            src_ref=src,
+            dst_ref=dst,
+            send_sem=send_sem.at[send],
+            recv_sem=recv,
+            device_id=to,
+            device_id_type=pl.DeviceIdType.MESH,
+        )
+
+    barrier = pltpu.get_barrier_semaphore()
+    senders = [
+        (beside, lat),
+        (across, lat),
+        (2 * (1 - probe) + other_half, lat),
+        (2 * probe, near),
+        (2 * probe + 1, near),
+    ]
+    for to in senders:
+        pl.semaphore_signal(
+            barrier, inc=1, device_id=to, device_id_type=pl.DeviceIdType.MESH
+        )
+    pl.semaphore_wait(barrier, len(senders))
+
+    inner = pl.ds(reach, band_rows)
+    far = remote(own_t.at[1], t_all.at[0, 1, :, inner], 0, far_sem.at[0], (across, lat))
+    far.start()
+    t_all[0, 0, :, inner] = own_t[0]
+    start[:, inner] = incident[:, probe].astype(jnp.bfloat16)
+
+    shared = pl.ds(pl.multiple_of(reach + (half_band - reach) * other_half, 16), half_band + reach)
+    edge_rows = pl.ds(pl.multiple_of((band_rows + reach) * half, 16), reach)
+    tail, head = pl.ds(band_rows, reach), pl.ds(reach, reach)
+    low, high = pl.ds(0, reach), pl.ds(band_rows + reach, reach)
+
+    def slot_copies(side):
+        return [
+            remote(
+                t_all.at[0, side, :, shared], t_all.at[1, side, :, shared],
+                1 + side, beside_sem.at[side], (beside, lat),
+            ),
+            remote(
+                t_all.at[0, side, :, tail], t_all.at[half, side, :, low],
+                3 + side, edge_sem.at[half, side], (2 * probe, after),
+            ),
+            remote(
+                t_all.at[0, side, :, head], t_all.at[other_half, side, :, high],
+                5 + side, edge_sem.at[other_half, side], (2 * probe + 1, before),
+            ),
+        ]
+
+    def finish_slot(side):
+        slot_copies(side)[0].wait_recv()
+        for core in range(2):
+            remote(
+                t_all.at[0, side, :, tail], t_all.at[core, side, :, edge_rows],
+                3, edge_sem.at[core, side], (beside, lat),
+            ).wait_recv()
+            edge = t_all[core, side, :, edge_rows]
+            t_all[core, side, :, edge_rows] = jnp.where(flags[2] != 0, edge, jnp.zeros_like(edge))
+
+    start_rows = pl.ds(pl.multiple_of(reach + (band_rows - reach) * other_half, 16), reach)
+    toward = lax.rem(lat + 1 - 2 * half + lat_count, lat_count)
+    start_copy = remote(
+        start.at[:, start_rows], start.at[:, edge_rows], 7, start_sem.at[0], (depth, toward)
+    )
+    near_copies = slot_copies(0)
+    for copy in [start_copy] + near_copies:
+        copy.start()
+
     re = [taps_ref[0, i] for i in range(tap_count)]
     im = [taps_ref[1, i] for i in range(tap_count)]
     ways = ((re, im), (re[::-1], [-tap for tap in im[::-1]]))
     for way, (tap_re, tap_im) in enumerate(ways):
         real = band(tap_re[::-1], rows, rows, 0, half_width)
         imag = band(tap_im[::-1], rows, rows, 0, half_width)
-        row_mat[way, :rows, :rows] = real.astype(jnp.bfloat16)
-        row_mat[way, :rows, rows:] = (-imag).astype(jnp.bfloat16)
-        row_mat[way, rows:, :rows] = imag.astype(jnp.bfloat16)
-        row_mat[way, rows:, rows:] = real.astype(jnp.bfloat16)
+        row_mat[way] = jnp.concatenate(
+            [
+                jnp.concatenate([real, -imag], axis=1),
+                jnp.concatenate([imag, real], axis=1),
+            ],
+            axis=0,
+        ).astype(jnp.bfloat16)
         real = band(tap_re, 384, 128, 128, half_width)
         imag = band(tap_im, 384, 128, 128, half_width)
         col_mat[way, :384, :128] = real.astype(jnp.bfloat16)
@@ -335,27 +431,80 @@
             for k in range(2)
         ]
 
+    extent = pl.ds(pl.multiple_of(half_band * half, 16), rows)
+
+    def place_of(s):
+        return lax.rem(s % 2 + half, 2), lax.rem(s // 2 + probe, 2)
+
     def factor(s):
-        core, side = lax.rem(s + half, 2), lax.rem(s // 2 + probe, 2)
-        return [
-            jnp.where(core == 0, keep[side, k], recv[side, k]).astype(jnp.float32)
-            for k in range(2)
-        ]
-
-    wave = [wave_ref[0], wave_ref[1]]
+        core, side = place_of(s)
+        both = t_all[core, side, :, extent].astype(jnp.float32)
+        return both[0], both[1]
+
+    def relay():
+        far.wait_recv()
+        for copy in slot_copies(1):
+            copy.start()
+        finish_slot(1)
+
+    start_copy.wait_recv()
+    finish_slot(0)
+    pl.when(probe == 1)(relay)
+    waves[0] = start[:, extent]
+    wave = None
     for s in range(slices):
-        waves[s, 0], waves[s, 1] = wave
+        if s == slices // 2:
+            pl.when(probe == 0)(relay)
         t_re, t_im = factor(s)
-        w_re, w_im = [part.astype(jnp.float32) for part in wave]
+        w_re, w_im = waves[s, 0].astype(jnp.float32), waves[s, 1].astype(jnp.float32)
         product = jnp.concatenate([t_re * w_re - t_im * w_im, t_re * w_im + t_im * w_re], axis=0)
         wave = cols_conv(rows_conv(product.astype(jnp.bfloat16), 0), 0)
-
-    w_re, w_im = [part.astype(jnp.float32) for part in wave]
-    window_row = base + lax.broadcasted_iota(jnp.int32, (rows, window), 0)
-    inside = (window_row >= 0) & (window_row < window)
-    residual = 2.0 * (w_re * w_re + w_im * w_im - meas_ref[...])
-    residual = jnp.where(inside, residual, 0.0)
-    adjoint = [(residual * w_re).astype(jnp.bfloat16), (residual * w_im).astype(jnp.bfloat16)]
+        if s + 1 < slices:
+            waves[s + 1, 0], waves[s + 1, 1] = wave
+
+    own = slice(reach, rows - reach)
+    w_re, w_im = [part[own].astype(jnp.float32) for part in wave]
+    own_rows = pl.ds(pl.multiple_of(half_band * half, 16), half_band)
+    residual = 2.0 * (w_re * w_re + w_im * w_im - measured[probe, own_rows])
+    adj[0, own] = (residual * w_re).astype(jnp.bfloat16)
+    adj[1, own] = (residual * w_im).astype(jnp.bfloat16)
+    up_lat = lax.rem(lat + half + lat_count - 1, lat_count)
+    down_lat = lax.rem(lat + half, lat_count)
+    adj_copies = [
+        remote(
+            adj.at[:, pl.ds(reach, reach)], adj.at[:, pl.ds(rows - reach, reach)],
+            8, adj_sem.at[1], (beside, up_lat),
+        ),
+        remote(
+            adj.at[:, pl.ds(rows - 2 * reach, reach)], adj.at[:, pl.ds(0, reach)],
+            9, adj_sem.at[0], (beside, down_lat),
+        ),
+    ]
+    for copy in adj_copies:
+        copy.start()
+    for copy in adj_copies:
+        copy.wait_recv()
+    adjoint = []
+    for k in range(2):
+        top, bottom = adj[k, :reach], adj[k, rows - reach :]
+        adjoint.append(
+            jnp.concatenate(
+                [
+                    jnp.where(flags[0] != 0, top, jnp.zeros_like(top)),
+                    adj[k, own],
+                    jnp.where(flags[1] != 0, bottom, jnp.zeros_like(bottom)),
+                ],
+                axis=0,
+            )
+        )
+
+    def term_copy(s):
+        core, side = place_of(s)
+        at = 2 * side + core
+        return remote(
+            terms.at[s], out_ref.at[side, core], 10 + at, term_sem.at[at], (s, lat)
+        )
+
     for s in reversed(range(slices)):
         spread = cols_conv(jnp.concatenate(adjoint, axis=0), 1)
         grad = rows_conv(jnp.concatenate(spread, axis=0), 1).astype(jnp.float32)
@@ -363,31 +512,59 @@
         t_re, t_im = factor(s)
         back_re = t_re * g_re + t_im * g_im
         back_im = t_re * g_im - t_im * g_re
-        own = slice(reach, rows - reach)
         e_re = waves[s, 0, own].astype(jnp.float32)
         e_im = waves[s, 1, own].astype(jnp.float32)
-        core, side = lax.rem(s + half, 2), lax.rem(s // 2 + probe, 2)
-        out_ref[core, side, 0] = (e_re * back_im[own] - e_im * back_re[own]).astype(jnp.bfloat16)
-        out_ref[core, side, 1] = (-e_re * back_re[own] - e_im * back_im[own]).astype(jnp.bfloat16)
+        terms[s, 0] = (e_re * back_im[own] - e_im * back_re[own]).astype(jnp.bfloat16)
+        terms[s, 1] = (-e_re * back_re[own] - e_im * back_im[own]).astype(jnp.bfloat16)
+        pl.when(depth != s)(lambda: term_copy(s).start())
+
+        @pl.when(depth == s)
+        def _():
+            out_ref[0, 0] = terms[s]
+
         adjoint = [back_re.astype(jnp.bfloat16), back_im.astype(jnp.bfloat16)]
 
-
-def section_terms(scalars, taps, keep, recv, wave, meas, half_band):
-    slices, rows, window = 4, meas.shape[0], meas.shape[1]
+    for copy in [far, start_copy] + near_copies + slot_copies(1) + adj_copies:
+        copy.wait_send()
+    for s in range(slices):
+        pl.when(depth != s)(lambda: term_copy(s).wait_send())
+    for at in range(1, 4):
+        remote(
+            terms.at[0], out_ref.at[at // 2, at % 2], 10 + at, term_sem.at[at], (beside, lat)
+        ).wait_recv()
+
+
+def section_terms(flags, taps, own_t, incident, measured, reach):
+    slices, band_rows, window = 4, own_t.shape[2], own_t.shape[3]
+    half_band = band_rows // 2
+    rows = half_band + 2 * reach
     smem = pl.BlockSpec(memory_space=pltpu.SMEM)
     vmem = pl.BlockSpec(memory_space=pltpu.VMEM)
     return pl.pallas_call(
         main_kernel,
         out_shape=jax.ShapeDtypeStruct((2, 2, 2, half_band, window), jnp.bfloat16),
-        in_specs=[smem, smem, vmem, vmem, vmem, vmem],
+        in_specs=[smem, smem, vmem, vmem, vmem],
         out_specs=vmem,
         scratch_shapes=[
+            pltpu.VMEM((2, 2, 2, band_rows + 2 * reach, window), jnp.bfloat16),
+            pltpu.VMEM((2, band_rows + 2 * reach, window), jnp.bfloat16),
             pltpu.VMEM((slices, 2, rows, window), jnp.bfloat16),
+            pltpu.VMEM((2, rows, window), jnp.bfloat16),
+            pltpu.VMEM((slices, 2, half_band, window), jnp.bfloat16),
             pltpu.VMEM((2, 2 * rows, 2 * rows), jnp.bfloat16),
             pltpu.VMEM((2, 768, 256), jnp.bfloat16),
+            pltpu.SemaphoreType.DMA((14,)),
+            pltpu.SemaphoreType.DMA((1,)),
+            pltpu.SemaphoreType.DMA((2,)),
+            pltpu.SemaphoreType.DMA((2, 2)),
+            pltpu.SemaphoreType.DMA((1,)),
+            pltpu.SemaphoreType.DMA((2,)),
+            pltpu.SemaphoreType.DMA((4,)),
         ],
-        compiler_params=pltpu.CompilerParams(vmem_limit_bytes=48 * 1024 * 1024),
-    )(scalars, taps, keep, recv, wave, meas)
+        compiler_params=pltpu.CompilerParams(
+            vmem_limit_bytes=48 * 1024 * 1024, collective_id=0, has_side_effects=True
+        ),
+    )(flags, taps, own_t, incident, measured)
 
 
 def place_kernel(scalars, own_ref, other_ref, out_ref):
@@ -433,8 +610,7 @@
     window = incident.shape[3]
     half_width = (kernel.shape[1] - 1) // 2
     half_band = band_rows // 2
-    reach = 8 * half_width
-    rows = half_band + 2 * reach
+    reach = 4 * half_width
     probe, half = depth_index // 2, depth_index % 2
     order = jnp.stack([probe, 1 - probe])
     first_band = offsets[:, 0][order] // band_rows
@@ -443,54 +619,11 @@
     scalars = jnp.concatenate([own_layer, offsets[:, 1][order], half[None]]).astype(jnp.int32)
 
     own_t = transmissions(scalars, potential[:, 0], window)
-    up = [(i, (i + 1) % lat_count) for i in range(lat_count)]
-    down = [((i + 1) % lat_count, i) for i in range(lat_count)]
-    above = lax.ppermute(own_t[:, :, band_rows - reach :], "lat", up)
-    below = lax.ppermute(own_t[:, :, :reach], "lat", down)
-    none = jnp.zeros((), jnp.bfloat16)
-    above = jnp.where((place_band > 0)[:, None, None, None], above, none)
-    below = jnp.where((place_band < lat_count - 1)[:, None, None, None], below, none)
-    ext_t = jnp.concatenate([above, own_t, below], axis=2)
-
-    across = [(i, i ^ 2) for i in range(4)]
-    beside = [(i, i ^ 1) for i in range(4)]
-    far_t = lax.ppermute(ext_t[1], "depth", across)
-    both_t = jnp.stack([ext_t[0], far_t])
-    keep_t = lax.dynamic_slice_in_dim(both_t, half * half_band, rows, 2)
-    send_t = lax.dynamic_slice_in_dim(both_t, (1 - half) * half_band, rows, 2)
-    recv_t = lax.ppermute(send_t, "depth", beside)
-
-    ring = []
-    for d in range(4):
-        for i in range(lat_count):
-            to = (i + 1) % lat_count if d % 2 == 0 else (i - 1) % lat_count
-            ring.append((d * lat_count + i, d * lat_count + to))
-
-    def extended(array):
-        axis = array.ndim - 2
-        tail = lax.slice_in_dim(array, band_rows - reach, band_rows, axis=axis)
-        front = lax.slice_in_dim(array, 0, reach, axis=axis)
-        edge = lax.ppermute(jnp.where(half == 0, tail, front), ("depth", "lat"), ring)
-        kept = rows - reach
-        low = jnp.concatenate([edge, lax.slice_in_dim(array, 0, kept, axis=axis)], axis)
-        high = jnp.concatenate(
-            [lax.slice_in_dim(array, band_rows - kept, band_rows, axis=axis), edge], axis
-        )
-        return jnp.where(half == 0, low, high)
-
-    wave = extended(
-        lax.dynamic_index_in_dim(incident, probe, 1, keepdims=False).astype(jnp.bfloat16)
-    )
-    meas = extended(lax.dynamic_index_in_dim(measured, probe, 0, keepdims=False))
-
-    base = place_band[0] * band_rows + half * half_band - reach
-    facts = jnp.stack([base, half, probe]).astype(jnp.int32)
-    terms = section_terms(
-        facts, kernel.astype(jnp.float32), keep_t, recv_t, wave, meas, half_band
-    )
-    joined = jnp.stack([terms[0], lax.ppermute(terms[1], "depth", beside)], axis=1)
-    other = lax.ppermute(joined[1], "depth", across)
-    return placed(scalars, joined[0], other, columns)[:, None]
+    top_ok = (half == 1) | (place_band[0] > 0)
+    bottom_ok = (half == 0) | (place_band[0] < lat_count - 1)
+    flags = jnp.stack([top_ok, bottom_ok, top_ok & bottom_ok]).astype(jnp.int32)
+    terms = section_terms(flags, kernel.astype(jnp.float32), own_t, incident, measured, reach)
+    return placed(scalars, terms[0], terms[1], columns)[:, None]
 
 
 def solution(mesh):

time: 99.7 us -> 65.3 us (0.65)
  waiting for transfers between devices: 43.4 us -> 0 us
  Pallas kernels: 25.2 us -> 58.6 us
  starting transfers between devices: 10.3 us -> 0 us
  other arithmetic: 9.59 us -> 1.58 us
  local copies, waits for them, and re-layouts: 10.4 us -> 4.54 us
    ppermute x8 -> x0, waiting for transfers between devices: 43.4 us -> none  [the longest x1 14.8 us: local_fast(): far_t = lax.ppermute(ext_t[1], 'depth', across)]
    pallas_call x1, Pallas kernels: 10.2 us -> 45.4 us  [section_terms(): pl.pallas_call(main_kernel, out_shape=jax.ShapeDtypeStruct((2, 2, 2, half...]
    ppermute x8 -> x0, starting transfers between devices: 10.3 us -> none  [the longest x1 3.1 us: local_fast(): below = lax.ppermute(own_t[:, :, :reach], 'lat', down)]
    select_n x6 -> x0, other arithmetic: 5.04 us -> none  [the longest x2 2.56 us: extended(): return jnp.where(half == 0, low, high)]
    slice x3 -> x0, local copies, waits for them, and re-layouts: 4.14 us -> none  [the longest x2 2.99 us: extended(): lax.slice_in_dim(array, band_rows - kept, band_rows, axis=axis)]
    another operation x2 -> x0, other arithmetic: 2.81 us -> none  [the longest x1 2.73 us: local_fast(): both_t = jnp.stack([ext_t[0], far_t])]
    pallas_call x1, Pallas kernels: 9.59 us -> 7.88 us  [transmissions(): pl.pallas_call(transmission_kernel, out_shape=jax.ShapeDtypeStruct((2, 2,...]
    unnamed x14 -> x6, local copies, waits for them, and re-layouts: 2.54 us -> 1.23 us
  transfers between devices with their start and end apart: 8 -> 0, of which waited for: 6 -> 0; matrix products, arithmetic and copies ran while one was open for 11% -> 0% of each run, Pallas kernels for 0% -> 0%
where the time goes in v2:
time: 65.3 us; the launch traced here: 64.9 us
  Pallas kernels  58.6 us (90%)
  local copies, waits for them, and re-layouts  4.54 us (7%)
  other arithmetic  1.58 us (2%)
    pallas_call x1, Pallas kernels, section_terms(): pl.pallas_call(main_kernel, out_shape=jax.ShapeDtypeStruct((2, 2, 2, half...  45.4 us
    pallas_call x1, Pallas kernels, transmissions(): pl.pallas_call(transmission_kernel, out_shape=jax.ShapeDtypeStruct((2, 2,...  7.88 us
    pallas_call x1, Pallas kernels, placed(): pl.pallas_call(place_kernel, out_shape=jax.ShapeDtypeStruct((2, 2, 2 * ha...  5.38 us

profile of v2, /device:TPU:0, one launch (start us, length us, event | category | flops | bytes accessed | tf_op | source)
XLA Modules:
  0.0 64.9 jit_solution(15671128288074732558)
XLA Ops:
  0.0 0.0 copy-start.2
  0.0 0.0 copy-start.1
  0.0 0.1 fusion.1
  0.1 0.8 %convert_element_type.7.taps_ref = f32[2,9]{1,0:T(2,128)S(1)} convert(bf16[2,9]{1,0:T(2,128)(2,1)} %param.9) | non-fusion elementwise | flops 18 | bytes 108 | tf_op jit(solution)/shard_map/convert_element_type | solution.py:625
  0.9 1.0 %slice_reduce_fusion.1 = (s32[2]{0:T(128)S(1)}, s32[2]{0:T(128)S(1)}) fusion(s32[2,2]{1,0:T(2,128)} %param.8), kind=kLoop, calls=%fused_computation.19 | loop fusion | bytes 32 | tf_op jit(solution)/shard_map/slice | solution.py:616
  1.9 0.6 gather_fusion.1
  2.5 0.6 gather_fusion
  3.3 0.1 add_convert_fusion.flags
  3.4 0.6 pad_add_fusion.scalars
  3.9 7.9 %shard_map.55.own_t = bf16[2,2,128,1024]{3,2,1,0:T(8,128)(2,1)} custom-call(s32[5]{0:T(128)} %pad_add_fusion.scalars, f32[2,2,128,2048]{3,2,1,0:T(8,128)} %bitcast.19), custom_call_target="tpu_custom_call" | custom-call | tf_op jit(solution)/shard_map/pallas_call | solution.py:268
  11.8 0.0 copy-done.2
  11.8 0.0 copy-done.1
  11.8 0.0 copy-start
  11.8 1.2 %copy-done = bf16[2,2,128,1024]{3,2,1,0:T(8,128)(2,1)S(1)} copy-done((bf16[2,2,128,1024]{3,2,1,0:T(8,128)(2,1)S(1)}, bf16[2,2,128,1024]{3,2,1,0:T(8,128)(2,1)}, u32[]{:S(2)}) %copy-start) | copy-done | bytes 1048600
  13.1 45.4 %shard_map.56 = bf16[2,2,2,64,1024]{4,3,2,1,0:T(8,128)(2,1)S(1)} custom-call(s32[3]{0:T(128)S(1)} %add_convert_fusion.flags, f32[2,9]{1,0:T(2,128)S(1)} %convert_element_type.7.taps_ref, bf16[2,2,128,1024]{3,2,1,0:T(8,128)(2,1)S(1)} %copy-done, f32[2,2,128,1024]{3,2,1,0:T(8,128)S(1)} %copy-done.1, f32[2,128,1024]{2,1,0:T(8,128)S(1)} %copy-done.2), custom_call_target="tpu_custom_call" | custom-call | tf_op jit(solution)/shard_map/pallas_call | solution.py:543
  58.4 1.1 %slice_bitcast_fusion = (bf16[2,2,64,1024]{3,2,1,0:T(8,128)(2,1)}, bf16[2,2,64,1024]{3,2,1,0:T(8,128)(2,1)}) fusion(bf16[2,2,2,64,1024]{4,3,2,1,0:T(8,128)(2,1)S(1)} %shard_map.56), kind=kLoop, calls=%fused_computation.2 | loop fusion | bytes 2097152 | tf_op jit(solution)/shard_map/squeeze | solution.py:626
  59.5 5.4 %shard_map.57 = f32[2,2,128,2048]{3,2,1,0:T(8,128)} custom-call(s32[5]{0:T(128)} %pad_add_fusion.scalars, bf16[2,2,64,1024]{3,2,1,0:T(8,128)(2,1)} %get-tuple-element.10.own_ref, bf16[2,2,64,1024]{3,2,1,0:T(8,128)(2,1)} %get-tuple-element.9.other_ref), custom_call_target="tpu_custom_call" | custom-call | tf_op jit(solution)/shard_map/pallas_call | solution.py:593
  (2 shorter events, 0.0 us)
Async XLA Ops:
  0.0 11.8 %copy-start.2 = (f32[2,128,1024]{2,1,0:T(8,128)S(1)}, f32[2,128,1024]{2,1,0:T(8,128)}, u32[]{:S(2)}) copy-start(f32[2,128,1024]{2,1,0:T(8,128)} %measured.1) | copy-start | bytes 3145732
  0.0 11.8 %copy-start.1 = (f32[2,2,128,1024]{3,2,1,0:T(8,128)S(1)}, f32[2,2,128,1024]{3,2,1,0:T(8,128)}, u32[]{:S(2)}) copy-start(f32[2,2,128,1024]{3,2,1,0:T(8,128)} %incident.1) | copy-start | bytes 6291460
  11.8 1.2 %copy-start = (bf16[2,2,128,1024]{3,2,1,0:T(8,128)(2,1)S(1)}, bf16[2,2,128,1024]{3,2,1,0:T(8,128)(2,1)}, u32[]{:S(2)}) copy-start(bf16[2,2,128,1024]{3,2,1,0:T(8,128)(2,1)} %shard_map.55.own_t) | copy-start | bytes 3145732

commit v3 on v2

--- a/solution.py
+++ b/solution.py
@@ -248,35 +248,61 @@
     return total
 
 
-def transmission_kernel(scalars, pot_ref, out_ref):
-    col = scalars[2 + pl.program_id(0)]
-    columns, window = pot_ref.shape[3], out_ref.shape[3]
-    shift = lax.rem(columns - col, columns)
-    phase = pltpu.roll(pot_ref[0, 0], shift, 1)[:, :window]
-    absorb = pltpu.roll(pot_ref[1, 0], shift, 1)[:, :window]
-    damping = jnp.exp(-absorb)
-    turn = 0.5 * phase
-    square = turn * turn
-    sine = turn * series(square, (1, -6, 120, -5040, 362880, -39916800, 6227020800))
-    cosine = series(square, (1, -2, 24, -720, 40320, -3628800, 479001600))
-    out_ref[0, 0] = (damping * (1.0 - 2.0 * sine * sine)).astype(out_ref.dtype)
-    out_ref[0, 1] = (2.0 * damping * sine * cosine).astype(out_ref.dtype)
-
-
-def transmissions(scalars, layer_pot, window):
-    band_rows, columns = layer_pot.shape[2:]
+def probe_place(offsets, probe, lat, lat_count, band_rows):
+    first_band = offsets[probe, 0] // band_rows
+    place_band = lax.rem(lat - first_band + lat_count, lat_count)
+    return place_band, (first_band + place_band) // lat_count, offsets[probe, 1]
+
+
+def write_transmission(pot, layer, col, row, dst, dst_row):
+    window = dst.shape[2]
+    last = pot.shape[3] // 128 - 1
+    block, lane = col // 128, lax.rem(col, 128)
+    turn_by = lax.rem(128 - lane, 128)
+    here = lax.broadcasted_iota(jnp.int32, (ROW_BLOCK, 128), 1) < 128 - lane
+    rows = pl.ds(row, ROW_BLOCK)
+
+    def turned(b):
+        at = pl.multiple_of(128 * jnp.minimum(block + b, last), 128)
+        return [pltpu.roll(pot[k, layer, rows, pl.ds(at, 128)], turn_by, 1) for k in range(2)]
+
+    low = turned(0)
+    for b in range(window // 128):
+        high = turned(b + 1)
+        phase, absorb = [jnp.where(here, low[k], high[k]) for k in range(2)]
+        damping = jnp.exp(-absorb)
+        turn = 0.5 * phase
+        square = turn * turn
+        sine = turn * series(square, (1, -6, 120, -5040, 362880, -39916800, 6227020800))
+        cosine = series(square, (1, -2, 24, -720, 40320, -3628800, 479001600))
+        at = pl.ds(128 * b, 128)
+        out_rows = pl.ds(dst_row, ROW_BLOCK)
+        dst[0, out_rows, at] = (damping * (1.0 - 2.0 * sine * sine)).astype(dst.dtype)
+        dst[1, out_rows, at] = (2.0 * damping * sine * cosine).astype(dst.dtype)
+        low = high
+
+
+def transmission_kernel(offsets, pot_ref, out_ref):
+    depth, lat = lax.axis_index("depth"), lax.axis_index("lat")
+    band_rows = ROW_BLOCK * pl.num_programs(0)
+    for q in range(2):
+        place = lax.rem(depth // 2 + q, 2)
+        _, layer, col = probe_place(offsets, place, lat, lax.axis_size("lat"), band_rows)
+        write_transmission(pot_ref, layer, col, 0, out_ref.at[q], 0)
+
+
+def transmissions(offsets, potential, window):
+    band_rows, columns = potential.shape[3:]
     return pl.pallas_call(
         transmission_kernel,
         out_shape=jax.ShapeDtypeStruct((2, 2, band_rows, window), jnp.bfloat16),
-        grid_spec=pltpu.PrefetchScalarGridSpec(
-            num_scalar_prefetch=1,
-            grid=(2, band_rows // ROW_BLOCK),
-            in_specs=[
-                pl.BlockSpec((2, 1, ROW_BLOCK, columns), lambda q, r, sc: (0, sc[q], r, 0))
-            ],
-            out_specs=pl.BlockSpec((1, 2, ROW_BLOCK, window), lambda q, r, sc: (q, 0, r, 0)),
-        ),
-    )(scalars, layer_pot)
+        grid=(band_rows // ROW_BLOCK,),
+        in_specs=[
+            pl.BlockSpec(memory_space=pltpu.SMEM),
+            pl.BlockSpec((2, 2, ROW_BLOCK, columns), lambda r: (0, 0, r, 0)),
+        ],
+        out_specs=pl.BlockSpec((2, 2, ROW_BLOCK, window), lambda r: (0, 0, r, 0)),
+    )(offsets, potential[:, 0])
 
 
 def band(taps, rows, cols, start, half_width):
@@ -293,14 +319,14 @@
 
 
 def main_kernel(
-    flags, taps_ref, own_t, incident, measured, out_ref,
-    t_all, start, waves, adj, terms, row_mat, col_mat,
-    send_sem, far_sem, beside_sem, edge_sem, start_sem, adj_sem, term_sem,
+    offsets, taps_ref, trans_hbm, incident_hbm, measured_hbm, out_ref,
+    incident, measured, far_t, t_all, start, waves, adj, terms, row_mat, col_mat,
+    send_sem, load_sem, far_sem, beside_sem, edge_sem, start_sem, adj_sem, term_sem,
 ):
     slices, _, rows, window = waves.shape
     tap_count = taps_ref.shape[1]
     half_width = (tap_count - 1) // 2
-    band_rows = own_t.shape[2]
+    band_rows = far_t.shape[1]
     half_band = band_rows // 2
     reach = (rows - half_band) // 2
     blocks = window // 128
@@ -323,6 +349,21 @@
             device_id_type=pl.DeviceIdType.MESH,
         )
 
+    own_rows = pl.ds(pl.multiple_of(half_band * half, 16), half_band)
+    loads = [
+        pltpu.make_async_copy(src, dst, load_sem.at[i])
+        for i, (src, dst) in enumerate(
+            [
+                (trans_hbm.at[1], far_t),
+                (trans_hbm.at[0], t_all.at[0, 0, :, pl.ds(reach, band_rows)]),
+                (incident_hbm.at[:, probe], incident),
+                (measured_hbm.at[probe, own_rows], measured),
+            ]
+        )
+    ]
+    for load in loads:
+        load.start()
+
     barrier = pltpu.get_barrier_semaphore()
     senders = [
         (beside, lat),
@@ -338,10 +379,19 @@
     pl.semaphore_wait(barrier, len(senders))
 
     inner = pl.ds(reach, band_rows)
-    far = remote(own_t.at[1], t_all.at[0, 1, :, inner], 0, far_sem.at[0], (across, lat))
+    place_row = band_rows * lat
+    at_row = offsets[probe, 0]
+    at_top = (at_row == place_row) | (at_row == place_row + window)
+    at_bottom = (at_row == place_row + band_rows) | (at_row == place_row + band_rows - window)
+    top_ok = jnp.logical_not(at_top) | (half == 1)
+    bottom_ok = jnp.logical_not(at_bottom) | (half == 0)
+
+    far = remote(far_t, t_all.at[0, 1, :, inner], 0, far_sem.at[0], (across, lat))
+    loads[0].wait()
     far.start()
-    t_all[0, 0, :, inner] = own_t[0]
-    start[:, inner] = incident[:, probe].astype(jnp.bfloat16)
+    loads[2].wait()
+    start[:, inner] = incident[...].astype(jnp.bfloat16)
+    loads[1].wait()
 
     shared = pl.ds(pl.multiple_of(reach + (half_band - reach) * other_half, 16), half_band + reach)
     edge_rows = pl.ds(pl.multiple_of((band_rows + reach) * half, 16), reach)
@@ -372,7 +422,7 @@
                 3, edge_sem.at[core, side], (beside, lat),
             ).wait_recv()
             edge = t_all[core, side, :, edge_rows]
-            t_all[core, side, :, edge_rows] = jnp.where(flags[2] != 0, edge, jnp.zeros_like(edge))
+            t_all[core, side, :, edge_rows] = jnp.where(top_ok & bottom_ok, edge, jnp.zeros_like(edge))
 
     start_rows = pl.ds(pl.multiple_of(reach + (band_rows - reach) * other_half, 16), reach)
     toward = lax.rem(lat + 1 - 2 * half + lat_count, lat_count)
@@ -383,8 +433,9 @@
     for copy in [start_copy] + near_copies:
         copy.start()
 
-    re = [taps_ref[0, i] for i in range(tap_count)]
-    im = [taps_ref[1, i] for i in range(tap_count)]
+    taps = taps_ref[...].astype(jnp.float32)
+    re = [taps[0:1, i : i + 1] for i in range(tap_count)]
+    im = [taps[1:2, i : i + 1] for i in range(tap_count)]
     ways = ((re, im), (re[::-1], [-tap for tap in im[::-1]]))
     for way, (tap_re, tap_im) in enumerate(ways):
         real = band(tap_re[::-1], rows, rows, 0, half_width)
@@ -464,8 +515,8 @@
 
     own = slice(reach, rows - reach)
     w_re, w_im = [part[own].astype(jnp.float32) for part in wave]
-    own_rows = pl.ds(pl.multiple_of(half_band * half, 16), half_band)
-    residual = 2.0 * (w_re * w_re + w_im * w_im - measured[probe, own_rows])
+    loads[3].wait()
+    residual = 2.0 * (w_re * w_re + w_im * w_im - measured[...])
     adj[0, own] = (residual * w_re).astype(jnp.bfloat16)
     adj[1, own] = (residual * w_im).astype(jnp.bfloat16)
     up_lat = lax.rem(lat + half + lat_count - 1, lat_count)
@@ -490,9 +541,9 @@
         adjoint.append(
             jnp.concatenate(
                 [
-                    jnp.where(flags[0] != 0, top, jnp.zeros_like(top)),
+                    jnp.where(top_ok, top, jnp.zeros_like(top)),
                     adj[k, own],
-                    jnp.where(flags[1] != 0, bottom, jnp.zeros_like(bottom)),
+                    jnp.where(bottom_ok, bottom, jnp.zeros_like(bottom)),
                 ],
                 axis=0,
             )
@@ -502,7 +553,7 @@
         core, side = place_of(s)
         at = 2 * side + core
         return remote(
-            terms.at[s], out_ref.at[side, core], 10 + at, term_sem.at[at], (s, lat)
+            terms.at[s], out_ref.at[side, core], 9 + at, term_sem.at[at], (s, lat)
         )
 
     for s in reversed(range(slices)):
@@ -530,22 +581,26 @@
         pl.when(depth != s)(lambda: term_copy(s).wait_send())
     for at in range(1, 4):
         remote(
-            terms.at[0], out_ref.at[at // 2, at % 2], 10 + at, term_sem.at[at], (beside, lat)
+            terms.at[0], out_ref.at[at // 2, at % 2], 9 + at, term_sem.at[at], (beside, lat)
         ).wait_recv()
 
 
-def section_terms(flags, taps, own_t, incident, measured, reach):
-    slices, band_rows, window = 4, own_t.shape[2], own_t.shape[3]
+def section_terms(offsets, taps, trans, incident, measured, reach):
+    slices, band_rows, window = 4, trans.shape[2], trans.shape[3]
     half_band = band_rows // 2
     rows = half_band + 2 * reach
     smem = pl.BlockSpec(memory_space=pltpu.SMEM)
     vmem = pl.BlockSpec(memory_space=pltpu.VMEM)
+    hbm = pl.BlockSpec(memory_space=pl.ANY)
     return pl.pallas_call(
         main_kernel,
         out_shape=jax.ShapeDtypeStruct((2, 2, 2, half_band, window), jnp.bfloat16),
-        in_specs=[smem, smem, vmem, vmem, vmem],
+        in_specs=[smem, vmem, hbm, hbm, hbm],
         out_specs=vmem,
         scratch_shapes=[
+            pltpu.VMEM((2, band_rows, window), jnp.float32),
+            pltpu.VMEM((half_band, window), jnp.float32),
+            pltpu.VMEM((2, band_rows, window), jnp.bfloat16),
             pltpu.VMEM((2, 2, 2, band_rows + 2 * reach, window), jnp.bfloat16),
             pltpu.VMEM((2, band_rows + 2 * reach, window), jnp.bfloat16),
             pltpu.VMEM((slices, 2, rows, window), jnp.bfloat16),
@@ -553,7 +608,8 @@
             pltpu.VMEM((slices, 2, half_band, window), jnp.bfloat16),
             pltpu.VMEM((2, 2 * rows, 2 * rows), jnp.bfloat16),
             pltpu.VMEM((2, 768, 256), jnp.bfloat16),
-            pltpu.SemaphoreType.DMA((14,)),
+            pltpu.SemaphoreType.DMA((13,)),
+            pltpu.SemaphoreType.DMA((4,)),
             pltpu.SemaphoreType.DMA((1,)),
             pltpu.SemaphoreType.DMA((2,)),
             pltpu.SemaphoreType.DMA((2, 2)),
@@ -564,66 +620,57 @@
         compiler_params=pltpu.CompilerParams(
             vmem_limit_bytes=48 * 1024 * 1024, collective_id=0, has_side_effects=True
         ),
-    )(flags, taps, own_t, incident, measured)
-
-
-def place_kernel(scalars, own_ref, other_ref, out_ref):
-    columns, window = out_ref.shape[3], own_ref.shape[3]
-    for part in range(2):
-        totals = [None, None]
-        for q, ref in enumerate((own_ref, other_ref)):
-            values = ref[0, part].astype(jnp.float32)
-            wide = jnp.concatenate([values, jnp.zeros_like(values)], axis=1)
-            wide = pltpu.roll(wide, scalars[2 + q], 1)
-            for layer in range(2):
-                term = jnp.where(scalars[q] == layer, wide, 0.0)
-                totals[layer] = term if q == 0 else totals[layer] + term
-        for layer in range(2):
-            out_ref[part, layer] = totals[layer]
-
-
-def placed(scalars, own, other, columns):
-    half_band, window = own.shape[2:]
+    )(offsets, taps, trans, incident, measured)
+
+
+def place_kernel(offsets, terms_ref, out_ref):
+    columns, window = out_ref.shape[3], terms_ref.shape[4]
+    half_band = terms_ref.shape[3]
     per_half = half_band // ROW_BLOCK
-
-    def pick(r, sc):
-        return (lax.rem(r // per_half + sc[4], 2), 0, lax.rem(r, per_half), 0)
-
-    spec = pl.BlockSpec((1, 2, ROW_BLOCK, window), pick)
+    depth, lat = lax.axis_index("depth"), lax.axis_index("lat")
+    probe, half = depth // 2, lax.rem(depth, 2)
+    r = pl.program_id(0)
+    core = lax.rem(r // per_half + half, 2)
+    rows = pl.ds(pl.multiple_of(ROW_BLOCK * lax.rem(r, per_half), ROW_BLOCK), ROW_BLOCK)
+    last = columns // 128 - 1
+    lanes = lax.broadcasted_iota(jnp.int32, (ROW_BLOCK, 128), 1)
+    out_ref[...] = jnp.zeros_like(out_ref)
+    for q in range(2):
+        place = lax.rem(probe + q, 2)
+        _, layer, col = probe_place(offsets, place, lat, lax.axis_size("lat"), 2 * half_band)
+        block, lane = col // 128, lax.rem(col, 128)
+        for part in range(2):
+            low = jnp.zeros((ROW_BLOCK, 128), jnp.float32)
+            for b in range(window // 128 + 1):
+                high = jnp.zeros((ROW_BLOCK, 128), jnp.float32)
+                if b < window // 128:
+                    values = terms_ref[q, core, part, rows, pl.ds(128 * b, 128)]
+                    high = pltpu.roll(values.astype(jnp.float32), lane, 1)
+                piece = jnp.where(lanes < lane, low, high)
+                at = pl.ds(pl.multiple_of(128 * jnp.minimum(block + b, last), 128), 128)
+                out_ref[part, layer, :, at] += piece
+                low = high
+
+
+def placed(offsets, terms, columns):
+    half_band = terms.shape[3]
     return pl.pallas_call(
         place_kernel,
         out_shape=jax.ShapeDtypeStruct((2, 2, 2 * half_band, columns), jnp.float32),
-        grid_spec=pltpu.PrefetchScalarGridSpec(
-            num_scalar_prefetch=1,
-            grid=(2 * per_half,),
-            in_specs=[spec, spec],
-            out_specs=pl.BlockSpec((2, 2, ROW_BLOCK, columns), lambda r, sc: (0, 0, r, 0)),
-        ),
-    )(scalars, own, other)
+        grid=(2 * half_band // ROW_BLOCK,),
+        in_specs=[
+            pl.BlockSpec(memory_space=pltpu.SMEM),
+            pl.BlockSpec(terms.shape, lambda r: (0, 0, 0, 0, 0)),
+        ],
+        out_specs=pl.BlockSpec((2, 2, ROW_BLOCK, columns), lambda r: (0, 0, r, 0)),
+    )(offsets, terms)
 
 
 def local_fast(potential, incident, measured, offsets, kernel):
-    lat_count = lax.axis_size("lat")
-    lat_index = lax.axis_index("lat")
-    depth_index = lax.axis_index("depth")
-    band_rows, columns = potential.shape[3:]
-    window = incident.shape[3]
-    half_width = (kernel.shape[1] - 1) // 2
-    half_band = band_rows // 2
-    reach = 4 * half_width
-    probe, half = depth_index // 2, depth_index % 2
-    order = jnp.stack([probe, 1 - probe])
-    first_band = offsets[:, 0][order] // band_rows
-    place_band = (lat_index - first_band) % lat_count
-    own_layer = (first_band + place_band) // lat_count
-    scalars = jnp.concatenate([own_layer, offsets[:, 1][order], half[None]]).astype(jnp.int32)
-
-    own_t = transmissions(scalars, potential[:, 0], window)
-    top_ok = (half == 1) | (place_band[0] > 0)
-    bottom_ok = (half == 0) | (place_band[0] < lat_count - 1)
-    flags = jnp.stack([top_ok, bottom_ok, top_ok & bottom_ok]).astype(jnp.int32)
-    terms = section_terms(flags, kernel.astype(jnp.float32), own_t, incident, measured, reach)
-    return placed(scalars, terms[0], terms[1], columns)[:, None]
+    reach = 4 * ((kernel.shape[1] - 1) // 2)
+    trans = transmissions(offsets, potential, incident.shape[3])
+    terms = section_terms(offsets, kernel, trans, incident, measured, reach)
+    return placed(offsets, terms, potential.shape[4])[:, None]
 
 
 def solution(mesh):

time: 65.3 us -> 57.2 us (0.88)
  Pallas kernels: 58.6 us -> 54.8 us
  local copies, waits for them, and re-layouts: 4.54 us -> 2.2 us
  other arithmetic: 1.58 us -> 0 us
    pallas_call x1, Pallas kernels: 7.88 us -> 5.06 us  [transmissions(): pl.pallas_call(transmission_kernel, out_shape=jax.ShapeDtypeStruct((2, 2,...]
    pallas_call x1, Pallas kernels: 5.38 us -> 4.07 us  [placed(): pl.pallas_call(place_kernel, out_shape=jax.ShapeDtypeStruct((2, 2, 2 * ha...]
    gather x2 -> x0, local copies, waits for them, and re-layouts: 1.28 us -> none  [the longest x1 0.64 us: local_fast(): offsets[:, 1][order]]
    squeeze x1 -> x0, local copies, waits for them, and re-layouts: 1.06 us -> none  [local_fast(): return placed(scalars, terms[0], terms[1], columns)[:, None]]
    slice x1 -> x0, local copies, waits for them, and re-layouts: 0.98 us -> none  [local_fast(): first_band = offsets[:, 0][order] // band_rows]
    unnamed x6 -> x12, local copies, waits for them, and re-layouts: 1.23 us -> 2.2 us
    convert_element_type x2 -> x0, other arithmetic: 0.88 us -> none  [the longest x1 0.81 us: local_fast(): kernel.astype(jnp.float32)]
where the time goes in v3:
time: 57.2 us; the launch traced here: 57 us
  Pallas kernels  54.8 us (96%)
  local copies, waits for them, and re-layouts  2.2 us (4%)
    pallas_call x1, Pallas kernels, section_terms(): pl.pallas_call(main_kernel, out_shape=jax.ShapeDtypeStruct((2, 2, 2, half...  45.6 us
    pallas_call x1, Pallas kernels, transmissions(): pl.pallas_call(transmission_kernel, out_shape=jax.ShapeDtypeStruct((2, 2,...  5.06 us
    pallas_call x1, Pallas kernels, placed(): pl.pallas_call(place_kernel, out_shape=jax.ShapeDtypeStruct((2, 2, 2 * ha...  4.07 us
    unnamed x12, local copies, waits for them, and re-layouts  2.2 us

profile of v3, /device:TPU:0, one launch (start us, length us, event | category | flops | bytes accessed | tf_op | source)
XLA Modules:
  0.0 57.0 jit_solution(17521180326561095767)
XLA Ops:
  0.0 0.0 copy-start.4
  0.0 0.0 copy-start.5
  0.0 0.0 copy-start.3
  0.0 0.0 copy-start.2
  0.0 5.1 %shard_map.55.trans_hbm = bf16[2,2,128,1024]{3,2,1,0:T(8,128)(2,1)} custom-call(s32[2,2]{1,0:T(2,128)} %offsets.5, f32[2,2,128,2048]{3,2,1,0:T(8,128)} %bitcast.4), custom_call_target="tpu_custom_call" | custom-call | tf_op jit(solution)/shard_map/pallas_call | solution.py:296
  5.1 0.0 copy-done.4
  5.1 0.0 copy-done.5
  5.1 0.0 copy-done.3
  5.1 0.0 copy-done.2
  5.1 0.0 copy-start.1
  5.1 1.2 %copy-done.1 = bf16[2,2,128,1024]{3,2,1,0:T(8,128)(2,1)S(1)} copy-done((bf16[2,2,128,1024]{3,2,1,0:T(8,128)(2,1)S(1)}, bf16[2,2,128,1024]{3,2,1,0:T(8,128)(2,1)}, u32[]{:S(2)}) %copy-start.1) | copy-done | bytes 1048600
  6.3 45.6 %shard_map.56.terms_ref = bf16[2,2,2,64,1024]{4,3,2,1,0:T(8,128)(2,1)S(1)} custom-call(s32[2,2]{1,0:T(2,128)S(1)} %copy-done.4, bf16[2,9]{1,0:T(2,128)(2,1)S(1)} %copy-done.5, bf16[2,2,128,1024]{3,2,1,0:T(8,128)(2,1)S(1)} %copy-done.1, f32[2,2,128,1024]{3,2,1,0:T(8,128)S(1)} %copy-done.2, f32[2,128,1024]{2,1,0:T(8,128)S(1)} %copy-done.3), custom_call_target="tpu_custom_call" | custom-call | tf_op jit(solution)/shard_map/pallas_call | solution.py:595
  52.0 0.0 copy-start
  52.0 1.0 %copy-done = bf16[2,2,2,64,1024]{4,3,2,1,0:T(8,128)(2,1)} copy-done((bf16[2,2,2,64,1024]{4,3,2,1,0:T(8,128)(2,1)}, bf16[2,2,2,64,1024]{4,3,2,1,0:T(8,128)(2,1)S(1)}, u32[]{:S(2)}) %copy-start) | copy-done | bytes 1048600
  52.9 4.1 %shard_map.57 = f32[2,2,128,2048]{3,2,1,0:T(8,128)} custom-call(s32[2,2]{1,0:T(2,128)} %offsets.5, bf16[2,2,2,64,1024]{4,3,2,1,0:T(8,128)(2,1)} %copy-done), custom_call_target="tpu_custom_call" | custom-call | tf_op jit(solution)/shard_map/pallas_call | solution.py:657
Async XLA Ops:
  0.0 5.1 %copy-start.4 = (s32[2,2]{1,0:T(2,128)S(1)}, s32[2,2]{1,0:T(2,128)}, u32[]{:S(2)}) copy-start(s32[2,2]{1,0:T(2,128)} %offsets.5) | copy-start | bytes 52
  0.0 5.1 %copy-start.5 = (bf16[2,9]{1,0:T(2,128)(2,1)S(1)}, bf16[2,9]{1,0:T(2,128)(2,1)}, u32[]{:S(2)}) copy-start(bf16[2,9]{1,0:T(2,128)(2,1)} %taps_ref.1) | copy-start | bytes 112
  0.0 5.1 %copy-start.3 = (f32[2,128,1024]{2,1,0:T(8,128)S(1)}, f32[2,128,1024]{2,1,0:T(8,128)}, u32[]{:S(2)}) copy-start(f32[2,128,1024]{2,1,0:T(8,128)} %measured_hbm.1) | copy-start | bytes 3145732
  0.0 5.1 %copy-start.2 = (f32[2,2,128,1024]{3,2,1,0:T(8,128)S(1)}, f32[2,2,128,1024]{3,2,1,0:T(8,128)}, u32[]{:S(2)}) copy-start(f32[2,2,128,1024]{3,2,1,0:T(8,128)} %incident_hbm.1) | copy-start | bytes 6291460
  5.1 1.2 %copy-start.1 = (bf16[2,2,128,1024]{3,2,1,0:T(8,128)(2,1)S(1)}, bf16[2,2,128,1024]{3,2,1,0:T(8,128)(2,1)}, u32[]{:S(2)}) copy-start(bf16[2,2,128,1024]{3,2,1,0:T(8,128)(2,1)} %shard_map.55.trans_hbm) | copy-start | bytes 3145732
  52.0 1.0 %copy-start = (bf16[2,2,2,64,1024]{4,3,2,1,0:T(8,128)(2,1)}, bf16[2,2,2,64,1024]{4,3,2,1,0:T(8,128)(2,1)S(1)}, u32[]{:S(2)}) copy-start(bf16[2,2,2,64,1024]{4,3,2,1,0:T(8,128)(2,1)S(1)} %shard_map.56.terms_ref) | copy-start | bytes 3145732

commit v4 on v3

--- a/solution.py
+++ b/solution.py
@@ -236,7 +236,8 @@
         and 2 * reach <= half_band
         and reach % 16 == 0
         and half_band % ROW_BLOCK == 0
-        and window % 128 == 0
+        and window % 256 == 0
+        and 8 * half_width <= 128
         and columns == 2 * window
     )
 
@@ -323,13 +324,15 @@
     incident, measured, far_t, t_all, start, waves, adj, terms, row_mat, col_mat,
     send_sem, load_sem, far_sem, beside_sem, edge_sem, start_sem, adj_sem, term_sem,
 ):
-    slices, _, rows, window = waves.shape
+    slices, _, rows, width = waves.shape
+    window = incident.shape[2]
+    share = window // 2
     tap_count = taps_ref.shape[1]
     half_width = (tap_count - 1) // 2
     band_rows = far_t.shape[1]
     half_band = band_rows // 2
     reach = (rows - half_band) // 2
-    blocks = window // 128
+    blocks = width // 128
     depth, lat = lax.axis_index("depth"), lax.axis_index("lat")
     lat_count = lax.axis_size("lat")
     probe, half = depth // 2, lax.rem(depth, 2)
@@ -386,9 +389,17 @@
     top_ok = jnp.logical_not(at_top) | (half == 1)
     bottom_ok = jnp.logical_not(at_bottom) | (half == 0)
 
-    far = remote(far_t, t_all.at[0, 1, :, inner], 0, far_sem.at[0], (across, lat))
+    fresh = [pl.ds(0, width), pl.ds(width, window - width)]
+    first = [0, window - width]
+    far = [
+        remote(
+            far_t.at[:, :, cols], t_all.at[0, 1, :, inner, cols],
+            13 + n, far_sem.at[n], (across, lat),
+        )
+        for n, cols in enumerate(fresh)
+    ]
     loads[0].wait()
-    far.start()
+    far[0].start()
     loads[2].wait()
     start[:, inner] = incident[...].astype(jnp.bfloat16)
     loads[1].wait()
@@ -398,36 +409,42 @@
     tail, head = pl.ds(band_rows, reach), pl.ds(reach, reach)
     low, high = pl.ds(0, reach), pl.ds(band_rows + reach, reach)
 
-    def slot_copies(side):
+    groups = [(0, pl.ds(0, window)), (1, fresh[0]), (1, fresh[1])]
+
+    def slot_copies(group):
+        side, cols = groups[group]
         return [
             remote(
-                t_all.at[0, side, :, shared], t_all.at[1, side, :, shared],
-                1 + side, beside_sem.at[side], (beside, lat),
+                t_all.at[0, side, :, shared, cols], t_all.at[1, side, :, shared, cols],
+                3 * group, beside_sem.at[group], (beside, lat),
             ),
             remote(
-                t_all.at[0, side, :, tail], t_all.at[half, side, :, low],
-                3 + side, edge_sem.at[half, side], (2 * probe, after),
+                t_all.at[0, side, :, tail, cols], t_all.at[half, side, :, low, cols],
+                3 * group + 1, edge_sem.at[half, group], (2 * probe, after),
             ),
             remote(
-                t_all.at[0, side, :, head], t_all.at[other_half, side, :, high],
-                5 + side, edge_sem.at[other_half, side], (2 * probe + 1, before),
+                t_all.at[0, side, :, head, cols], t_all.at[other_half, side, :, high, cols],
+                3 * group + 2, edge_sem.at[other_half, group], (2 * probe + 1, before),
             ),
         ]
 
-    def finish_slot(side):
-        slot_copies(side)[0].wait_recv()
+    def finish_slot(group):
+        side, cols = groups[group]
+        slot_copies(group)[0].wait_recv()
         for core in range(2):
             remote(
-                t_all.at[0, side, :, tail], t_all.at[core, side, :, edge_rows],
-                3, edge_sem.at[core, side], (beside, lat),
+                t_all.at[0, side, :, tail, cols], t_all.at[core, side, :, edge_rows, cols],
+                3 * group + 1, edge_sem.at[core, group], (beside, lat),
             ).wait_recv()
-            edge = t_all[core, side, :, edge_rows]
-            t_all[core, side, :, edge_rows] = jnp.where(top_ok & bottom_ok, edge, jnp.zeros_like(edge))
+            edge = t_all[core, side, :, edge_rows, cols]
+            t_all[core, side, :, edge_rows, cols] = jnp.where(
+                top_ok & bottom_ok, edge, jnp.zeros_like(edge)
+            )
 
     start_rows = pl.ds(pl.multiple_of(reach + (band_rows - reach) * other_half, 16), reach)
     toward = lax.rem(lat + 1 - 2 * half + lat_count, lat_count)
     start_copy = remote(
-        start.at[:, start_rows], start.at[:, edge_rows], 7, start_sem.at[0], (depth, toward)
+        start.at[:, start_rows], start.at[:, edge_rows], 9, start_sem.at[0], (depth, toward)
     )
     near_copies = slot_copies(0)
     for copy in [start_copy] + near_copies:
@@ -487,108 +504,133 @@
     def place_of(s):
         return lax.rem(s % 2 + half, 2), lax.rem(s // 2 + probe, 2)
 
-    def factor(s):
+    def factor(s, cols):
         core, side = place_of(s)
-        both = t_all[core, side, :, extent].astype(jnp.float32)
+        both = t_all[core, side, :, extent, cols].astype(jnp.float32)
         return both[0], both[1]
 
-    def relay():
-        far.wait_recv()
-        for copy in slot_copies(1):
-            copy.start()
-        finish_slot(1)
-
+    def term_copy(n, s):
+        core, side = place_of(s)
+        at = 2 * side + core
+        cols = pl.ds(share * n, share)
+        return remote(
+            terms.at[s, :, :, cols], out_ref.at[side, core, :, :, cols],
+            15 + 4 * n + at, term_sem.at[n, at], (s, lat),
+        )
+
+    def adjoint_copies(n):
+        return [
+            remote(
+                adj.at[n, :, pl.ds(reach, reach)], adj.at[n, :, pl.ds(rows - reach, reach)],
+                23 + n, adj_sem.at[n, 1], (beside, up_lat),
+            ),
+            remote(
+                adj.at[n, :, pl.ds(rows - 2 * reach, reach)], adj.at[n, :, pl.ds(0, reach)],
+                25 + n, adj_sem.at[n, 0], (beside, down_lat),
+            ),
+        ]
+
+    up_lat = lax.rem(lat + half + lat_count - 1, lat_count)
+    down_lat = lax.rem(lat + half, lat_count)
+    own = slice(reach, rows - reach)
+    far[0].wait_send()
+    far[1].start()
+    far[0].wait_recv()
+    for copy in slot_copies(1):
+        copy.start()
     start_copy.wait_recv()
     finish_slot(0)
-    pl.when(probe == 1)(relay)
-    waves[0] = start[:, extent]
-    wave = None
-    for s in range(slices):
-        if s == slices // 2:
-            pl.when(probe == 0)(relay)
-        t_re, t_im = factor(s)
-        w_re, w_im = waves[s, 0].astype(jnp.float32), waves[s, 1].astype(jnp.float32)
-        product = jnp.concatenate([t_re * w_re - t_im * w_im, t_re * w_im + t_im * w_re], axis=0)
-        wave = cols_conv(rows_conv(product.astype(jnp.bfloat16), 0), 0)
-        if s + 1 < slices:
-            waves[s + 1, 0], waves[s + 1, 1] = wave
-
-    own = slice(reach, rows - reach)
-    w_re, w_im = [part[own].astype(jnp.float32) for part in wave]
-    loads[3].wait()
-    residual = 2.0 * (w_re * w_re + w_im * w_im - measured[...])
-    adj[0, own] = (residual * w_re).astype(jnp.bfloat16)
-    adj[1, own] = (residual * w_im).astype(jnp.bfloat16)
-    up_lat = lax.rem(lat + half + lat_count - 1, lat_count)
-    down_lat = lax.rem(lat + half, lat_count)
-    adj_copies = [
-        remote(
-            adj.at[:, pl.ds(reach, reach)], adj.at[:, pl.ds(rows - reach, reach)],
-            8, adj_sem.at[1], (beside, up_lat),
-        ),
-        remote(
-            adj.at[:, pl.ds(rows - 2 * reach, reach)], adj.at[:, pl.ds(0, reach)],
-            9, adj_sem.at[0], (beside, down_lat),
-        ),
-    ]
-    for copy in adj_copies:
-        copy.start()
-    for copy in adj_copies:
-        copy.wait_recv()
-    adjoint = []
-    for k in range(2):
-        top, bottom = adj[k, :reach], adj[k, rows - reach :]
-        adjoint.append(
-            jnp.concatenate(
-                [
-                    jnp.where(top_ok, top, jnp.zeros_like(top)),
-                    adj[k, own],
-                    jnp.where(bottom_ok, bottom, jnp.zeros_like(bottom)),
-                ],
-                axis=0,
+
+    for n in range(2):
+        cols = pl.ds(first[n], width)
+        if n == 0:
+            pl.when(probe == 1)(lambda: finish_slot(1))
+        else:
+            finish_slot(2)
+        waves[0] = start[:, extent, cols]
+        wave = None
+        for s in range(slices):
+            if s == slices // 2 and n == 0:
+                pl.when(probe == 0)(lambda: finish_slot(1))
+            t_re, t_im = factor(s, cols)
+            w_re, w_im = waves[s, 0].astype(jnp.float32), waves[s, 1].astype(jnp.float32)
+            product = jnp.concatenate(
+                [t_re * w_re - t_im * w_im, t_re * w_im + t_im * w_re], axis=0
             )
-        )
-
-    def term_copy(s):
-        core, side = place_of(s)
-        at = 2 * side + core
-        return remote(
-            terms.at[s], out_ref.at[side, core], 9 + at, term_sem.at[at], (s, lat)
-        )
-
-    for s in reversed(range(slices)):
-        spread = cols_conv(jnp.concatenate(adjoint, axis=0), 1)
-        grad = rows_conv(jnp.concatenate(spread, axis=0), 1).astype(jnp.float32)
-        g_re, g_im = grad[:rows], grad[rows:]
-        t_re, t_im = factor(s)
-        back_re = t_re * g_re + t_im * g_im
-        back_im = t_re * g_im - t_im * g_re
-        e_re = waves[s, 0, own].astype(jnp.float32)
-        e_im = waves[s, 1, own].astype(jnp.float32)
-        terms[s, 0] = (e_re * back_im[own] - e_im * back_re[own]).astype(jnp.bfloat16)
-        terms[s, 1] = (-e_re * back_re[own] - e_im * back_im[own]).astype(jnp.bfloat16)
-        pl.when(depth != s)(lambda: term_copy(s).start())
-
-        @pl.when(depth == s)
-        def _():
-            out_ref[0, 0] = terms[s]
-
-        adjoint = [back_re.astype(jnp.bfloat16), back_im.astype(jnp.bfloat16)]
-
-    for copy in [far, start_copy] + near_copies + slot_copies(1) + adj_copies:
+            wave = cols_conv(rows_conv(product.astype(jnp.bfloat16), 0), 0)
+            if s + 1 < slices:
+                waves[s + 1, 0], waves[s + 1, 1] = wave
+
+        w_re, w_im = [part[own].astype(jnp.float32) for part in wave]
+        if n == 0:
+            loads[3].wait()
+        residual = 2.0 * (w_re * w_re + w_im * w_im - measured[:, cols])
+        adj[n, 0, own] = (residual * w_re).astype(jnp.bfloat16)
+        adj[n, 1, own] = (residual * w_im).astype(jnp.bfloat16)
+        for copy in adjoint_copies(n):
+            copy.start()
+        if n == 0:
+            far[1].wait_recv()
+            for copy in slot_copies(2):
+                copy.start()
+        for copy in adjoint_copies(n):
+            copy.wait_recv()
+        adjoint = []
+        for k in range(2):
+            top, bottom = adj[n, k, :reach], adj[n, k, rows - reach :]
+            adjoint.append(
+                jnp.concatenate(
+                    [
+                        jnp.where(top_ok, top, jnp.zeros_like(top)),
+                        adj[n, k, own],
+                        jnp.where(bottom_ok, bottom, jnp.zeros_like(bottom)),
+                    ],
+                    axis=0,
+                )
+            )
+
+        mine = slice(share * n - first[n], share * n - first[n] + share)
+        kept = slice(share * n, share * n + share)
+        for s in reversed(range(slices)):
+            spread = cols_conv(jnp.concatenate(adjoint, axis=0), 1)
+            grad = rows_conv(jnp.concatenate(spread, axis=0), 1).astype(jnp.float32)
+            g_re, g_im = grad[:rows], grad[rows:]
+            t_re, t_im = factor(s, cols)
+            back_re = t_re * g_re + t_im * g_im
+            back_im = t_re * g_im - t_im * g_re
+            b_re, b_im = back_re[own, mine], back_im[own, mine]
+            e_re = waves[s, 0, own, mine].astype(jnp.float32)
+            e_im = waves[s, 1, own, mine].astype(jnp.float32)
+            terms[s, 0, :, kept] = (e_re * b_im - e_im * b_re).astype(jnp.bfloat16)
+            terms[s, 1, :, kept] = (-e_re * b_re - e_im * b_im).astype(jnp.bfloat16)
+            pl.when(depth != s)(lambda: term_copy(n, s).start())
+
+            @pl.when(depth == s)
+            def _():
+                out_ref[0, 0, :, :, kept] = terms[s, :, :, kept]
+
+            adjoint = [back_re.astype(jnp.bfloat16), back_im.astype(jnp.bfloat16)]
+
+    for copy in [far[1], start_copy] + near_copies + slot_copies(1) + slot_copies(2):
         copy.wait_send()
-    for s in range(slices):
-        pl.when(depth != s)(lambda: term_copy(s).wait_send())
-    for at in range(1, 4):
-        remote(
-            terms.at[0], out_ref.at[at // 2, at % 2], 9 + at, term_sem.at[at], (beside, lat)
-        ).wait_recv()
+    for n in range(2):
+        for copy in adjoint_copies(n):
+            copy.wait_send()
+        for s in range(slices):
+            pl.when(depth != s)(lambda: term_copy(n, s).wait_send())
+        cols = pl.ds(share * n, share)
+        for at in range(1, 4):
+            remote(
+                terms.at[0, :, :, cols], out_ref.at[at // 2, at % 2, :, :, cols],
+                15 + 4 * n + at, term_sem.at[n, at], (beside, lat),
+            ).wait_recv()
 
 
 def section_terms(offsets, taps, trans, incident, measured, reach):
     slices, band_rows, window = 4, trans.shape[2], trans.shape[3]
     half_band = band_rows // 2
     rows = half_band + 2 * reach
+    width = window // 2 + 128
     smem = pl.BlockSpec(memory_space=pltpu.SMEM)
     vmem = pl.BlockSpec(memory_space=pltpu.VMEM)
     hbm = pl.BlockSpec(memory_space=pl.ANY)
@@ -603,22 +645,22 @@
             pltpu.VMEM((2, band_rows, window), jnp.bfloat16),
             pltpu.VMEM((2, 2, 2, band_rows + 2 * reach, window), jnp.bfloat16),
             pltpu.VMEM((2, band_rows + 2 * reach, window), jnp.bfloat16),
-            pltpu.VMEM((slices, 2, rows, window), jnp.bfloat16),
-            pltpu.VMEM((2, rows, window), jnp.bfloat16),
+            pltpu.VMEM((slices, 2, rows, width), jnp.bfloat16),
+            pltpu.VMEM((2, 2, rows, width), jnp.bfloat16),
             pltpu.VMEM((slices, 2, half_band, window), jnp.bfloat16),
             pltpu.VMEM((2, 2 * rows, 2 * rows), jnp.bfloat16),
             pltpu.VMEM((2, 768, 256), jnp.bfloat16),
-            pltpu.SemaphoreType.DMA((13,)),
+            pltpu.SemaphoreType.DMA((27,)),
             pltpu.SemaphoreType.DMA((4,)),
+            pltpu.SemaphoreType.DMA((2,)),
+            pltpu.SemaphoreType.DMA((3,)),
+            pltpu.SemaphoreType.DMA((2, 3)),
             pltpu.SemaphoreType.DMA((1,)),
-            pltpu.SemaphoreType.DMA((2,)),
             pltpu.SemaphoreType.DMA((2, 2)),
-            pltpu.SemaphoreType.DMA((1,)),
-            pltpu.SemaphoreType.DMA((2,)),
-            pltpu.SemaphoreType.DMA((4,)),
+            pltpu.SemaphoreType.DMA((2, 4)),
         ],
         compiler_params=pltpu.CompilerParams(
-            vmem_limit_bytes=48 * 1024 * 1024, collective_id=0, has_side_effects=True
+            vmem_limit_bytes=60 * 1024 * 1024, collective_id=0, has_side_effects=True
         ),
     )(offsets, taps, trans, incident, measured)
 

time: 57.2 us -> 53.4 us (0.934)
  local copies, waits for them, and re-layouts: 2.2 us -> 0 us
  Pallas kernels: 54.8 us -> 53.2 us
    unnamed x12 -> x0, local copies, waits for them, and re-layouts: 2.2 us -> none
    pallas_call x1, Pallas kernels: 45.6 us -> 44.2 us  [section_terms(): pl.pallas_call(main_kernel, out_shape=jax.ShapeDtypeStruct((2, 2, 2, half...]
where the time goes in v4:
time: 53.4 us; the launch traced here: 53.2 us
  Pallas kernels  53.2 us (100%)
    pallas_call x1, Pallas kernels, section_terms(): pl.pallas_call(main_kernel, out_shape=jax.ShapeDtypeStruct((2, 2, 2, half...  44.2 us
    pallas_call x1, Pallas kernels, transmissions(): pl.pallas_call(transmission_kernel, out_shape=jax.ShapeDtypeStruct((2, 2,...  4.9 us
    pallas_call x1, Pallas kernels, placed(): pl.pallas_call(place_kernel, out_shape=jax.ShapeDtypeStruct((2, 2, 2 * ha...  4.11 us

profile of v4, /device:TPU:0, one launch (start us, length us, event | category | flops | bytes accessed | tf_op | source)
XLA Modules:
  0.0 53.2 jit_solution(12321035639339122881)
XLA Ops:
  0.0 4.9 %shard_map.55.trans_hbm = bf16[2,2,128,1024]{3,2,1,0:T(8,128)(2,1)} custom-call(s32[2,2]{1,0:T(2,128)} %offsets.5, f32[2,2,128,2048]{3,2,1,0:T(8,128)} %bitcast.4), custom_call_target="tpu_custom_call" | custom-call | tf_op jit(solution)/shard_map/pallas_call | solution.py:297
  4.9 44.2 %shard_map.56.terms_ref = bf16[2,2,2,64,1024]{4,3,2,1,0:T(8,128)(2,1)} custom-call(s32[2,2]{1,0:T(2,128)} %offsets.5, bf16[2,9]{1,0:T(2,128)(2,1)} %taps_ref.1, bf16[2,2,128,1024]{3,2,1,0:T(8,128)(2,1)} %shard_map.55.trans_hbm, f32[2,2,128,1024]{3,2,1,0:T(8,128)} %incident_hbm.1, f32[2,128,1024]{2,1,0:T(8,128)} %measured_hbm.1), custom_call_target="tpu_custom_call" | custom-call | tf_op jit(solution)/shard_map/pallas_call | solution.py:637
  49.1 4.1 %shard_map.57 = f32[2,2,128,2048]{3,2,1,0:T(8,128)} custom-call(s32[2,2]{1,0:T(2,128)} %offsets.5, bf16[2,2,2,64,1024]{4,3,2,1,0:T(8,128)(2,1)} %shard_map.56.terms_ref), custom_call_target="tpu_custom_call" | custom-call | tf_op jit(solution)/shard_map/pallas_call | solution.py:699

commit v5 on v4

--- a/solution.py
+++ b/solution.py
@@ -267,20 +267,24 @@
         at = pl.multiple_of(128 * jnp.minimum(block + b, last), 128)
         return [pltpu.roll(pot[k, layer, rows, pl.ds(at, 128)], turn_by, 1) for k in range(2)]
 
-    low = turned(0)
-    for b in range(window // 128):
-        high = turned(b + 1)
-        phase, absorb = [jnp.where(here, low[k], high[k]) for k in range(2)]
+    blocks = [turned(b) for b in range(window // 128 + 1)]
+    for b in range(0, window // 128, 2):
+        phase, absorb = [
+            jnp.concatenate(
+                [jnp.where(here, blocks[i][k], blocks[i + 1][k]) for i in (b, b + 1)], axis=1
+            )
+            for k in range(2)
+        ]
         damping = jnp.exp(-absorb)
         turn = 0.5 * phase
         square = turn * turn
         sine = turn * series(square, (1, -6, 120, -5040, 362880, -39916800, 6227020800))
         cosine = series(square, (1, -2, 24, -720, 40320, -3628800, 479001600))
-        at = pl.ds(128 * b, 128)
+        at = pl.ds(128 * b, 256)
         out_rows = pl.ds(dst_row, ROW_BLOCK)
-        dst[0, out_rows, at] = (damping * (1.0 - 2.0 * sine * sine)).astype(dst.dtype)
-        dst[1, out_rows, at] = (2.0 * damping * sine * cosine).astype(dst.dtype)
-        low = high
+        bent = 2.0 * damping * sine
+        dst[0, out_rows, at] = (damping - bent * sine).astype(dst.dtype)
+        dst[1, out_rows, at] = (bent * cosine).astype(dst.dtype)
 
 
 def transmission_kernel(offsets, pot_ref, out_ref):
@@ -682,16 +686,19 @@
         _, layer, col = probe_place(offsets, place, lat, lax.axis_size("lat"), 2 * half_band)
         block, lane = col // 128, lax.rem(col, 128)
         for part in range(2):
-            low = jnp.zeros((ROW_BLOCK, 128), jnp.float32)
-            for b in range(window // 128 + 1):
-                high = jnp.zeros((ROW_BLOCK, 128), jnp.float32)
-                if b < window // 128:
-                    values = terms_ref[q, core, part, rows, pl.ds(128 * b, 128)]
-                    high = pltpu.roll(values.astype(jnp.float32), lane, 1)
-                piece = jnp.where(lanes < lane, low, high)
-                at = pl.ds(pl.multiple_of(128 * jnp.minimum(block + b, last), 128), 128)
-                out_ref[part, layer, :, at] += piece
-                low = high
+            turned = [jnp.zeros((ROW_BLOCK, 128), jnp.float32)]
+            for b in range(window // 128):
+                values = terms_ref[q, core, part, rows, pl.ds(128 * b, 128)]
+                turned.append(pltpu.roll(values.astype(jnp.float32), lane, 1))
+            pieces = [jnp.where(lanes < lane, low, high) for low, high in zip(turned, turned[1:])]
+            wide = jnp.concatenate(pieces, axis=1)
+            past = jnp.where(lanes < lane, turned[-1], 0.0)
+            at = pl.ds(pl.multiple_of(128 * block, 128), window)
+            end = pl.multiple_of(128 * jnp.minimum(block + window // 128, last), 128)
+            if q == 1:
+                wide = wide + out_ref[part, layer, :, at]
+            out_ref[part, layer, :, at] = wide
+            out_ref[part, layer, :, pl.ds(end, 128)] += past
 
 
 def placed(offsets, terms, columns):

time: 53.4 us -> 53.2 us (level)
  no operation moved by 1% of the time
where the time goes in v5:
time: 53.2 us; the launch traced here: 53 us
  Pallas kernels  53 us (100%)
    pallas_call x1, Pallas kernels, section_terms(): pl.pallas_call(main_kernel, out_shape=jax.ShapeDtypeStruct((2, 2, 2, half...  44.2 us
    pallas_call x1, Pallas kernels, transmissions(): pl.pallas_call(transmission_kernel, out_shape=jax.ShapeDtypeStruct((2, 2,...  4.84 us
    pallas_call x1, Pallas kernels, placed(): pl.pallas_call(place_kernel, out_shape=jax.ShapeDtypeStruct((2, 2, 2 * ha...  3.98 us

profile of v5, /device:TPU:0, one launch (start us, length us, event | category | flops | bytes accessed | tf_op | source)
XLA Modules:
  0.0 53.0 jit_solution(8725287228059549457)
XLA Ops:
  0.0 4.8 %shard_map.55.trans_hbm = bf16[2,2,128,1024]{3,2,1,0:T(8,128)(2,1)} custom-call(s32[2,2]{1,0:T(2,128)} %offsets.5, f32[2,2,128,2048]{3,2,1,0:T(8,128)} %bitcast.4), custom_call_target="tpu_custom_call" | custom-call | tf_op jit(solution)/shard_map/pallas_call | solution.py:301
  4.8 44.2 %shard_map.56.terms_ref = bf16[2,2,2,64,1024]{4,3,2,1,0:T(8,128)(2,1)} custom-call(s32[2,2]{1,0:T(2,128)} %offsets.5, bf16[2,9]{1,0:T(2,128)(2,1)} %taps_ref.1, bf16[2,2,128,1024]{3,2,1,0:T(8,128)(2,1)} %shard_map.55.trans_hbm, f32[2,2,128,1024]{3,2,1,0:T(8,128)} %incident_hbm.1, f32[2,128,1024]{2,1,0:T(8,128)} %measured_hbm.1), custom_call_target="tpu_custom_call" | custom-call | tf_op jit(solution)/shard_map/pallas_call | solution.py:641
  49.0 4.0 %shard_map.57 = f32[2,2,128,2048]{3,2,1,0:T(8,128)} custom-call(s32[2,2]{1,0:T(2,128)} %offsets.5, bf16[2,2,2,64,1024]{4,3,2,1,0:T(8,128)(2,1)} %shard_map.56.terms_ref), custom_call_target="tpu_custom_call" | custom-call | tf_op jit(solution)/shard_map/pallas_call | solution.py:706

commit v6 on v5

--- a/solution.py
+++ b/solution.py
@@ -255,17 +255,15 @@
     return place_band, (first_band + place_band) // lat_count, offsets[probe, 1]
 
 
-def write_transmission(pot, layer, col, row, dst, dst_row):
+def write_transmission(pot, block, lane, dst):
     window = dst.shape[2]
-    last = pot.shape[3] // 128 - 1
-    block, lane = col // 128, lax.rem(col, 128)
+    last = pot.shape[2] // 128 - 1
     turn_by = lax.rem(128 - lane, 128)
     here = lax.broadcasted_iota(jnp.int32, (ROW_BLOCK, 128), 1) < 128 - lane
-    rows = pl.ds(row, ROW_BLOCK)
 
     def turned(b):
         at = pl.multiple_of(128 * jnp.minimum(block + b, last), 128)
-        return [pltpu.roll(pot[k, layer, rows, pl.ds(at, 128)], turn_by, 1) for k in range(2)]
+        return [pltpu.roll(pot[k, :, pl.ds(at, 128)], turn_by, 1) for k in range(2)]
 
     blocks = [turned(b) for b in range(window // 128 + 1)]
     for b in range(0, window // 128, 2):
@@ -281,33 +279,63 @@
         sine = turn * series(square, (1, -6, 120, -5040, 362880, -39916800, 6227020800))
         cosine = series(square, (1, -2, 24, -720, 40320, -3628800, 479001600))
         at = pl.ds(128 * b, 256)
-        out_rows = pl.ds(dst_row, ROW_BLOCK)
         bent = 2.0 * damping * sine
-        dst[0, out_rows, at] = (damping - bent * sine).astype(dst.dtype)
-        dst[1, out_rows, at] = (bent * cosine).astype(dst.dtype)
-
-
-def transmission_kernel(offsets, pot_ref, out_ref):
+        dst[0, :, at] = (damping - bent * sine).astype(dst.dtype)
+        dst[1, :, at] = (bent * cosine).astype(dst.dtype)
+
+
+def transmission_kernel(offsets, pot_hbm, out_hbm, pot, out, in_sem, out_sem):
     depth, lat = lax.axis_index("depth"), lax.axis_index("lat")
-    band_rows = ROW_BLOCK * pl.num_programs(0)
+    chunks = pot.shape[1]
+    band_rows = ROW_BLOCK * chunks
+    columns, fetched = pot_hbm.shape[4], pot.shape[4]
+    places = []
     for q in range(2):
         place = lax.rem(depth // 2 + q, 2)
         _, layer, col = probe_place(offsets, place, lat, lax.axis_size("lat"), band_rows)
-        write_transmission(pot_ref, layer, col, 0, out_ref.at[q], 0)
+        places.append((layer, jnp.minimum(col // 128, (columns - fetched) // 128), col))
+
+    def copy_in(q, r):
+        layer, begin, _ = places[q]
+        cols = pl.ds(pl.multiple_of(128 * begin, 128), fetched)
+        src = pot_hbm.at[:, 0, layer, pl.ds(ROW_BLOCK * r, ROW_BLOCK), cols]
+        return pltpu.make_async_copy(src, pot.at[q, r], in_sem.at[q, r])
+
+    def copy_out(q, r):
+        dst = out_hbm.at[q, :, pl.ds(ROW_BLOCK * r, ROW_BLOCK)]
+        return pltpu.make_async_copy(out.at[q, r], dst, out_sem.at[q, r])
+
+    order = [(q, r) for q in range(2) for r in range(chunks)]
+    for q, r in order:
+        copy_in(q, r).start()
+    for q, r in order:
+        _, begin, col = places[q]
+        copy_in(q, r).wait()
+        write_transmission(pot.at[q, r], col // 128 - begin, lax.rem(col, 128), out.at[q, r])
+        copy_out(q, r).start()
+    for q, r in order:
+        copy_out(q, r).wait()
 
 
 def transmissions(offsets, potential, window):
-    band_rows, columns = potential.shape[3:]
+    band_rows = potential.shape[3]
+    chunks = band_rows // ROW_BLOCK
     return pl.pallas_call(
         transmission_kernel,
         out_shape=jax.ShapeDtypeStruct((2, 2, band_rows, window), jnp.bfloat16),
-        grid=(band_rows // ROW_BLOCK,),
         in_specs=[
             pl.BlockSpec(memory_space=pltpu.SMEM),
-            pl.BlockSpec((2, 2, ROW_BLOCK, columns), lambda r: (0, 0, r, 0)),
+            pl.BlockSpec(memory_space=pl.ANY),
         ],
-        out_specs=pl.BlockSpec((2, 2, ROW_BLOCK, window), lambda r: (0, 0, r, 0)),
-    )(offsets, potential[:, 0])
+        out_specs=pl.BlockSpec(memory_space=pl.ANY),
+        scratch_shapes=[
+            pltpu.VMEM((2, chunks, 2, ROW_BLOCK, window + 128), jnp.float32),
+            pltpu.VMEM((2, chunks, 2, ROW_BLOCK, window), jnp.bfloat16),
+            pltpu.SemaphoreType.DMA((2, chunks)),
+            pltpu.SemaphoreType.DMA((2, chunks)),
+        ],
+        compiler_params=pltpu.CompilerParams(vmem_limit_bytes=60 * 1024 * 1024),
+    )(offsets, potential)
 
 
 def band(taps, rows, cols, start, half_width):
@@ -669,18 +697,11 @@
     )(offsets, taps, trans, incident, measured)
 
 
-def place_kernel(offsets, terms_ref, out_ref):
-    columns, window = out_ref.shape[3], terms_ref.shape[4]
-    half_band = terms_ref.shape[3]
-    per_half = half_band // ROW_BLOCK
-    depth, lat = lax.axis_index("depth"), lax.axis_index("lat")
-    probe, half = depth // 2, lax.rem(depth, 2)
-    r = pl.program_id(0)
-    core = lax.rem(r // per_half + half, 2)
-    rows = pl.ds(pl.multiple_of(ROW_BLOCK * lax.rem(r, per_half), ROW_BLOCK), ROW_BLOCK)
+def place_rows(offsets, probe, lat, half_band, core_terms, out_ref):
+    columns, window = out_ref.shape[3], core_terms[0].shape[2]
+    out_ref[...] = jnp.zeros_like(out_ref)
     last = columns // 128 - 1
     lanes = lax.broadcasted_iota(jnp.int32, (ROW_BLOCK, 128), 1)
-    out_ref[...] = jnp.zeros_like(out_ref)
     for q in range(2):
         place = lax.rem(probe + q, 2)
         _, layer, col = probe_place(offsets, place, lat, lax.axis_size("lat"), 2 * half_band)
@@ -688,7 +709,7 @@
         for part in range(2):
             turned = [jnp.zeros((ROW_BLOCK, 128), jnp.float32)]
             for b in range(window // 128):
-                values = terms_ref[q, core, part, rows, pl.ds(128 * b, 128)]
+                values = core_terms[q][part, :, pl.ds(128 * b, 128)]
                 turned.append(pltpu.roll(values.astype(jnp.float32), lane, 1))
             pieces = [jnp.where(lanes < lane, low, high) for low, high in zip(turned, turned[1:])]
             wide = jnp.concatenate(pieces, axis=1)
@@ -701,17 +722,62 @@
             out_ref[part, layer, :, pl.ds(end, 128)] += past
 
 
+def place_kernel(offsets, terms_hbm, out_hbm, terms, out, in_sem, out_sem):
+    depth, lat = lax.axis_index("depth"), lax.axis_index("lat")
+    probe, half = depth // 2, lax.rem(depth, 2)
+    chunks, half_band = out.shape[0], terms_hbm.shape[3]
+    per_half = chunks // 2
+
+    def copy_in(q, r):
+        core = lax.rem(r // per_half + half, 2)
+        rows = pl.ds(ROW_BLOCK * (r % per_half), ROW_BLOCK)
+        src = terms_hbm.at[q, core, :, rows]
+        return pltpu.make_async_copy(src, terms.at[q, r], in_sem.at[q, r])
+
+    def copies_out(r):
+        rows = pl.ds(ROW_BLOCK * r, ROW_BLOCK)
+        return [
+            pltpu.make_async_copy(
+                out.at[r, part, layer],
+                out_hbm.at[part, 0, layer, rows],
+                out_sem.at[r, part, layer],
+            )
+            for part in range(2)
+            for layer in range(2)
+        ]
+
+    for r in range(chunks):
+        for q in range(2):
+            copy_in(q, r).start()
+    for r in range(chunks):
+        for q in range(2):
+            copy_in(q, r).wait()
+        place_rows(offsets, probe, lat, half_band, [terms.at[0, r], terms.at[1, r]], out.at[r])
+        for copy in copies_out(r):
+            copy.start()
+    for r in range(chunks):
+        for copy in copies_out(r):
+            copy.wait()
+
+
 def placed(offsets, terms, columns):
-    half_band = terms.shape[3]
+    half_band, window = terms.shape[3:]
+    chunks = 2 * half_band // ROW_BLOCK
     return pl.pallas_call(
         place_kernel,
-        out_shape=jax.ShapeDtypeStruct((2, 2, 2 * half_band, columns), jnp.float32),
-        grid=(2 * half_band // ROW_BLOCK,),
+        out_shape=jax.ShapeDtypeStruct((2, 1, 2, 2 * half_band, columns), jnp.float32),
         in_specs=[
             pl.BlockSpec(memory_space=pltpu.SMEM),
-            pl.BlockSpec(terms.shape, lambda r: (0, 0, 0, 0, 0)),
+            pl.BlockSpec(memory_space=pl.ANY),
         ],
-        out_specs=pl.BlockSpec((2, 2, ROW_BLOCK, columns), lambda r: (0, 0, r, 0)),
+        out_specs=pl.BlockSpec(memory_space=pl.ANY),
+        scratch_shapes=[
+            pltpu.VMEM((2, chunks, 2, ROW_BLOCK, window), jnp.bfloat16),
+            pltpu.VMEM((chunks, 2, 2, ROW_BLOCK, columns), jnp.float32),
+            pltpu.SemaphoreType.DMA((2, chunks)),
+            pltpu.SemaphoreType.DMA((chunks, 2, 2)),
+        ],
+        compiler_params=pltpu.CompilerParams(vmem_limit_bytes=60 * 1024 * 1024),
     )(offsets, terms)
 
 
@@ -719,7 +785,7 @@
     reach = 4 * ((kernel.shape[1] - 1) // 2)
     trans = transmissions(offsets, potential, incident.shape[3])
     terms = section_terms(offsets, kernel, trans, incident, measured, reach)
-    return placed(offsets, terms, potential.shape[4])[:, None]
+    return placed(offsets, terms, potential.shape[4])
 
 
 def solution(mesh):

time: 53.2 us -> 52.9 us (level)
  no operation moved by 1% of the time
where the time goes in v6:
time: 52.9 us; the launch traced here: 52.7 us
  Pallas kernels  52.7 us (100%)
    pallas_call x1, Pallas kernels, section_terms(): pl.pallas_call(main_kernel, out_shape=jax.ShapeDtypeStruct((2, 2, 2, half...  44.2 us
    pallas_call x1, Pallas kernels, transmissions(): pl.pallas_call(transmission_kernel, out_shape=jax.ShapeDtypeStruct((2, 2,...  4.47 us
    pallas_call x1, Pallas kernels, placed(): pl.pallas_call(place_kernel, out_shape=jax.ShapeDtypeStruct((2, 1, 2, 2 *...  4.03 us

profile of v6, /device:TPU:0, one launch (start us, length us, event | category | flops | bytes accessed | tf_op | source)
XLA Modules:
  0.0 52.7 jit_solution(15066931900125025418)
XLA Ops:
  0.0 4.5 %shard_map.55.trans_hbm = bf16[2,2,128,1024]{3,2,1,0:T(8,128)(2,1)} custom-call(s32[2,2]{1,0:T(2,128)} %offsets.5, f32[2,1,2,128,2048]{4,3,2,1,0:T(8,128)} %pot_hbm.1), custom_call_target="tpu_custom_call" | custom-call | tf_op jit(solution)/shard_map/pallas_call | solution.py:323
  4.5 44.2 %shard_map.56.terms_hbm = bf16[2,2,2,64,1024]{4,3,2,1,0:T(8,128)(2,1)} custom-call(s32[2,2]{1,0:T(2,128)} %offsets.5, bf16[2,9]{1,0:T(2,128)(2,1)} %taps_ref.1, bf16[2,2,128,1024]{3,2,1,0:T(8,128)(2,1)} %shard_map.55.trans_hbm, f32[2,2,128,1024]{3,2,1,0:T(8,128)} %incident_hbm.1, f32[2,128,1024]{2,1,0:T(8,128)} %measured_hbm.1), custom_call_target="tpu_custom_call" | custom-call | tf_op jit(solution)/shard_map/pallas_call | solution.py:669
  48.7 4.0 %shard_map.57 = f32[2,1,2,128,2048]{4,3,2,1,0:T(8,128)} custom-call(s32[2,2]{1,0:T(2,128)} %offsets.5, bf16[2,2,2,64,1024]{4,3,2,1,0:T(8,128)(2,1)} %shard_map.56.terms_hbm), custom_call_target="tpu_custom_call" | custom-call | tf_op jit(solution)/shard_map/pallas_call | solution.py:766

commit v7 on v6

--- a/solution.py
+++ b/solution.py
@@ -255,7 +255,17 @@
     return place_band, (first_band + place_band) // lat_count, offsets[probe, 1]
 
 
-def write_transmission(pot, block, lane, dst):
+def transmission(phase, absorb):
+    damping = jnp.exp(-absorb)
+    turn = 0.5 * phase
+    square = turn * turn
+    sine = turn * series(square, (1, -6, 120, -5040, 362880, -39916800, 6227020800))
+    cosine = series(square, (1, -2, 24, -720, 40320, -3628800, 479001600))
+    bent = 2.0 * damping * sine
+    return damping - bent * sine, bent * cosine
+
+
+def write_window(pot, block, lane, dst, convert):
     window = dst.shape[2]
     last = pot.shape[2] // 128 - 1
     turn_by = lax.rem(128 - lane, 128)
@@ -273,18 +283,12 @@
             )
             for k in range(2)
         ]
-        damping = jnp.exp(-absorb)
-        turn = 0.5 * phase
-        square = turn * turn
-        sine = turn * series(square, (1, -6, 120, -5040, 362880, -39916800, 6227020800))
-        cosine = series(square, (1, -2, 24, -720, 40320, -3628800, 479001600))
-        at = pl.ds(128 * b, 256)
-        bent = 2.0 * damping * sine
-        dst[0, :, at] = (damping - bent * sine).astype(dst.dtype)
-        dst[1, :, at] = (bent * cosine).astype(dst.dtype)
-
-
-def transmission_kernel(offsets, pot_hbm, out_hbm, pot, out, in_sem, out_sem):
+        values = transmission(phase, absorb) if convert else (phase, absorb)
+        for k in range(2):
+            dst[k, :, pl.ds(128 * b, 256)] = values[k].astype(dst.dtype)
+
+
+def transmission_kernel(offsets, pot_hbm, own_hbm, far_hbm, pot, own, far, in_sem, out_sem):
     depth, lat = lax.axis_index("depth"), lax.axis_index("lat")
     chunks = pot.shape[1]
     band_rows = ROW_BLOCK * chunks
@@ -302,8 +306,9 @@
         return pltpu.make_async_copy(src, pot.at[q, r], in_sem.at[q, r])
 
     def copy_out(q, r):
-        dst = out_hbm.at[q, :, pl.ds(ROW_BLOCK * r, ROW_BLOCK)]
-        return pltpu.make_async_copy(out.at[q, r], dst, out_sem.at[q, r])
+        src, dst = ((own, own_hbm), (far, far_hbm))[q]
+        dst = dst.at[:, pl.ds(ROW_BLOCK * r, ROW_BLOCK)]
+        return pltpu.make_async_copy(src.at[r], dst, out_sem.at[q, r])
 
     order = [(q, r) for q in range(2) for r in range(chunks)]
     for q, r in order:
@@ -311,7 +316,8 @@
     for q, r in order:
         _, begin, col = places[q]
         copy_in(q, r).wait()
-        write_transmission(pot.at[q, r], col // 128 - begin, lax.rem(col, 128), out.at[q, r])
+        dst = (own, far)[q].at[r]
+        write_window(pot.at[q, r], col // 128 - begin, lax.rem(col, 128), dst, q == 1)
         copy_out(q, r).start()
     for q, r in order:
         copy_out(q, r).wait()
@@ -322,15 +328,19 @@
     chunks = band_rows // ROW_BLOCK
     return pl.pallas_call(
         transmission_kernel,
-        out_shape=jax.ShapeDtypeStruct((2, 2, band_rows, window), jnp.bfloat16),
+        out_shape=[
+            jax.ShapeDtypeStruct((2, band_rows, window), jnp.float32),
+            jax.ShapeDtypeStruct((2, band_rows, window), jnp.bfloat16),
+        ],
         in_specs=[
             pl.BlockSpec(memory_space=pltpu.SMEM),
             pl.BlockSpec(memory_space=pl.ANY),
         ],
-        out_specs=pl.BlockSpec(memory_space=pl.ANY),
+        out_specs=[pl.BlockSpec(memory_space=pl.ANY)] * 2,
         scratch_shapes=[
             pltpu.VMEM((2, chunks, 2, ROW_BLOCK, window + 128), jnp.float32),
-            pltpu.VMEM((2, chunks, 2, ROW_BLOCK, window), jnp.bfloat16),
+            pltpu.VMEM((chunks, 2, ROW_BLOCK, window), jnp.float32),
+            pltpu.VMEM((chunks, 2, ROW_BLOCK, window), jnp.bfloat16),
             pltpu.SemaphoreType.DMA((2, chunks)),
             pltpu.SemaphoreType.DMA((2, chunks)),
         ],
@@ -352,8 +362,8 @@
 
 
 def main_kernel(
-    offsets, taps_ref, trans_hbm, incident_hbm, measured_hbm, out_ref,
-    incident, measured, far_t, t_all, start, waves, adj, terms, row_mat, col_mat,
+    offsets, taps_ref, own_hbm, far_hbm, incident_hbm, measured_hbm, out_ref,
+    incident, measured, own_raw, far_t, t_all, start, waves, adj, terms, row_mat, col_mat,
     send_sem, load_sem, far_sem, beside_sem, edge_sem, start_sem, adj_sem, term_sem,
 ):
     slices, _, rows, width = waves.shape
@@ -389,8 +399,8 @@
         pltpu.make_async_copy(src, dst, load_sem.at[i])
         for i, (src, dst) in enumerate(
             [
-                (trans_hbm.at[1], far_t),
-                (trans_hbm.at[0], t_all.at[0, 0, :, pl.ds(reach, band_rows)]),
+                (far_hbm, far_t),
+                (own_hbm, own_raw),
                 (incident_hbm.at[:, probe], incident),
                 (measured_hbm.at[probe, own_rows], measured),
             ]
@@ -435,6 +445,16 @@
     loads[2].wait()
     start[:, inner] = incident[...].astype(jnp.bfloat16)
     loads[1].wait()
+
+    @pl.loop(0, band_rows // 16)
+    def _(r):
+        rows_in = pl.ds(pl.multiple_of(16 * r, 16), 16)
+        rows_out = pl.ds(pl.multiple_of(reach + 16 * r, 16), 16)
+        for b in range(0, window, 256):
+            at = pl.ds(b, 256)
+            values = transmission(own_raw[0, rows_in, at], own_raw[1, rows_in, at])
+            t_all[0, 0, 0, rows_out, at] = values[0].astype(jnp.bfloat16)
+            t_all[0, 0, 1, rows_out, at] = values[1].astype(jnp.bfloat16)
 
     shared = pl.ds(pl.multiple_of(reach + (half_band - reach) * other_half, 16), half_band + reach)
     edge_rows = pl.ds(pl.multiple_of((band_rows + reach) * half, 16), reach)
@@ -658,8 +678,8 @@
             ).wait_recv()
 
 
-def section_terms(offsets, taps, trans, incident, measured, reach):
-    slices, band_rows, window = 4, trans.shape[2], trans.shape[3]
+def section_terms(offsets, taps, own, far, incident, measured, reach):
+    slices, band_rows, window = 4, far.shape[1], far.shape[2]
     half_band = band_rows // 2
     rows = half_band + 2 * reach
     width = window // 2 + 128
@@ -669,11 +689,12 @@
     return pl.pallas_call(
         main_kernel,
         out_shape=jax.ShapeDtypeStruct((2, 2, 2, half_band, window), jnp.bfloat16),
-        in_specs=[smem, vmem, hbm, hbm, hbm],
+        in_specs=[smem, vmem, hbm, hbm, hbm, hbm],
         out_specs=vmem,
         scratch_shapes=[
             pltpu.VMEM((2, band_rows, window), jnp.float32),
             pltpu.VMEM((half_band, window), jnp.float32),
+            pltpu.VMEM((2, band_rows, window), jnp.float32),
             pltpu.VMEM((2, band_rows, window), jnp.bfloat16),
             pltpu.VMEM((2, 2, 2, band_rows + 2 * reach, window), jnp.bfloat16),
             pltpu.VMEM((2, band_rows + 2 * reach, window), jnp.bfloat16),
@@ -694,7 +715,7 @@
         compiler_params=pltpu.CompilerParams(
             vmem_limit_bytes=60 * 1024 * 1024, collective_id=0, has_side_effects=True
         ),
-    )(offsets, taps, trans, incident, measured)
+    )(offsets, taps, own, far, incident, measured)
 
 
 def place_rows(offsets, probe, lat, half_band, core_terms, out_ref):
@@ -783,8 +804,8 @@
 
 def local_fast(potential, incident, measured, offsets, kernel):
     reach = 4 * ((kernel.shape[1] - 1) // 2)
-    trans = transmissions(offsets, potential, incident.shape[3])
-    terms = section_terms(offsets, kernel, trans, incident, measured, reach)
+    own, far = transmissions(offsets, potential, incident.shape[3])
+    terms = section_terms(offsets, kernel, own, far, incident, measured, reach)
     return placed(offsets, terms, potential.shape[4])
 
 

time: 52.9 us -> 52.5 us (level)
  no operation moved by 1% of the time
where the time goes in v7:
time: 52.5 us; the launch traced here: 52.3 us
  Pallas kernels  52.3 us (100%)
    pallas_call x1, Pallas kernels, section_terms(): pl.pallas_call(main_kernel, out_shape=jax.ShapeDtypeStruct((2, 2, 2, half...  44.2 us
    pallas_call x1, Pallas kernels, transmissions(): pl.pallas_call(transmission_kernel, out_shape=[jax.ShapeDtypeStruct((2, b...  4.06 us
    pallas_call x1, Pallas kernels, placed(): pl.pallas_call(place_kernel, out_shape=jax.ShapeDtypeStruct((2, 1, 2, 2 *...  4.03 us

profile of v7, /device:TPU:0, one launch (start us, length us, event | category | flops | bytes accessed | tf_op | source)
XLA Modules:
  0.0 52.3 jit_solution(7146857236477267489)
XLA Ops:
  0.0 4.1 %shard_map.55 = (f32[2,128,1024]{2,1,0:T(8,128)}, bf16[2,128,1024]{2,1,0:T(8,128)(2,1)}) custom-call(s32[2,2]{1,0:T(2,128)} %offsets.5, f32[2,1,2,128,2048]{4,3,2,1,0:T(8,128)} %pot_hbm.1), custom_call_target="tpu_custom_call" | custom-call | tf_op jit(solution)/shard_map/pallas_call | solution.py:329
  4.1 44.2 %shard_map.56.terms_hbm = bf16[2,2,2,64,1024]{4,3,2,1,0:T(8,128)(2,1)} custom-call(s32[2,2]{1,0:T(2,128)} %offsets.5, bf16[2,9]{1,0:T(2,128)(2,1)} %taps_ref.1, f32[2,128,1024]{2,1,0:T(8,128)} %get-tuple-element.7.own_hbm, bf16[2,128,1024]{2,1,0:T(8,128)(2,1)} %get-tuple-element.8.far_hbm, f32[2,2,128,1024]{3,2,1,0:T(8,128)} %incident_hbm.1, ...), custom_call_target="tpu_custom_call" | custom-call | tf_op jit(solution)/shard_map/pallas_call | solution.py:689
  48.3 4.0 %shard_map.57 = f32[2,1,2,128,2048]{4,3,2,1,0:T(8,128)} custom-call(s32[2,2]{1,0:T(2,128)} %offsets.5, bf16[2,2,2,64,1024]{4,3,2,1,0:T(8,128)(2,1)} %shard_map.56.terms_hbm), custom_call_target="tpu_custom_call" | custom-call | tf_op jit(solution)/shard_map/pallas_call | solution.py:787

commit v8 on v7

--- a/solution.py
+++ b/solution.py
@@ -442,6 +442,7 @@
     ]
     loads[0].wait()
     far[0].start()
+    far[1].start()
     loads[2].wait()
     start[:, inner] = incident[...].astype(jnp.bfloat16)
     loads[1].wait()
@@ -585,8 +586,6 @@
     up_lat = lax.rem(lat + half + lat_count - 1, lat_count)
     down_lat = lax.rem(lat + half, lat_count)
     own = slice(reach, rows - reach)
-    far[0].wait_send()
-    far[1].start()
     far[0].wait_recv()
     for copy in slot_copies(1):
         copy.start()
@@ -663,7 +662,7 @@
 
             adjoint = [back_re.astype(jnp.bfloat16), back_im.astype(jnp.bfloat16)]
 
-    for copy in [far[1], start_copy] + near_copies + slot_copies(1) + slot_copies(2):
+    for copy in far + [start_copy] + near_copies + slot_copies(1) + slot_copies(2):
         copy.wait_send()
     for n in range(2):
         for copy in adjoint_copies(n):

time: 52.5 us -> 53 us (level)
  no operation moved by 1% of the time
where the time goes in v8:
time: 53 us; the launch traced here: 52.8 us
  Pallas kernels  52.7 us (99%)
    pallas_call x1, Pallas kernels, section_terms(): pl.pallas_call(main_kernel, out_shape=jax.ShapeDtypeStruct((2, 2, 2, half...  44.6 us
    pallas_call x1, Pallas kernels, transmissions(): pl.pallas_call(transmission_kernel, out_shape=[jax.ShapeDtypeStruct((2, b...  4.06 us
    pallas_call x1, Pallas kernels, placed(): pl.pallas_call(place_kernel, out_shape=jax.ShapeDtypeStruct((2, 1, 2, 2 *...  4.03 us

profile of v8, /device:TPU:0, one launch (start us, length us, event | category | flops | bytes accessed | tf_op | source)
XLA Modules:
  0.0 52.8 jit_solution(15348014833108002209)
XLA Ops:
  0.0 4.1 %shard_map.55 = (f32[2,128,1024]{2,1,0:T(8,128)}, bf16[2,128,1024]{2,1,0:T(8,128)(2,1)}) custom-call(s32[2,2]{1,0:T(2,128)} %offsets.5, f32[2,1,2,128,2048]{4,3,2,1,0:T(8,128)} %pot_hbm.1), custom_call_target="tpu_custom_call" | custom-call | tf_op jit(solution)/shard_map/pallas_call | solution.py:329
  4.1 44.6 %shard_map.56.terms_hbm = bf16[2,2,2,64,1024]{4,3,2,1,0:T(8,128)(2,1)} custom-call(s32[2,2]{1,0:T(2,128)} %offsets.5, bf16[2,9]{1,0:T(2,128)(2,1)} %taps_ref.1, f32[2,128,1024]{2,1,0:T(8,128)} %get-tuple-element.7.own_hbm, bf16[2,128,1024]{2,1,0:T(8,128)(2,1)} %get-tuple-element.8.far_hbm, f32[2,2,128,1024]{3,2,1,0:T(8,128)} %incident_hbm.1, ...), custom_call_target="tpu_custom_call" | custom-call | tf_op jit(solution)/shard_map/pallas_call | solution.py:688
  48.7 4.0 %shard_map.57 = f32[2,1,2,128,2048]{4,3,2,1,0:T(8,128)} custom-call(s32[2,2]{1,0:T(2,128)} %offsets.5, bf16[2,2,2,64,1024]{4,3,2,1,0:T(8,128)(2,1)} %shard_map.56.terms_hbm), custom_call_target="tpu_custom_call" | custom-call | tf_op jit(solution)/shard_map/pallas_call | solution.py:786
